TPU v7x, 256 devices: a whole 4x4x8 slice. The times are simulated.
256 devices in a mesh: row: 8 (over y, z_hi), col: 32 (over x, z_lo, core).
Axes of the slice: x: 4, y: 4, z: 8 (z_hi: 2, z_lo: 4; z = z_hi * 4 + z_lo), core: 2. Of those that a mesh axis runs over, the one named last changes fastest.
Arguments:
- latent: float32 [4, 1024, 1024], P(None, 'col', 'row')
- row_offset: int32 [1], replicated, may hold values from 1 to 127
- col_offset: int32 [1], replicated, may hold values from 1 to 31
- timestep: int32 [1], replicated, may hold values from 0 to 999
- w_in: bfloat16 [9, 320, 4], replicated, may hold values from -1 to 1
- norm_gain: float32 [320], replicated, may hold values from 0.1 to 1.9
- norm_shift: float32 [320], replicated, may hold values from -3 to 3
- w_conv: bfloat16 [9, 320, 320], P(None, 'col'), may hold values from -0.109375 to 0.109375
- w_time1: bfloat16 [320, 1280], P(None, 'col'), may hold values from -0.3125 to 0.3125
- w_time2: bfloat16 [1280, 1280], P('col'), may hold values from -0.15625 to 0.15625
- w_time3: bfloat16 [1280, 320], P(None, 'col'), may hold values from -0.15625 to 0.15625
Outputs:
- conv_out: bfloat16 [320, 1024, 1024], P(None, 'col', 'row')
All inputs are finite; a program needn't handle non-finite values.
Results may differ from a plain program's by a relative error of at most 0.0057.
Values may be sent and summed in bfloat16 or wider, within the bound.
No kernel may reach another device: no remote copies, remote signals or barrier semaphores. Data moves between devices by JAX's collectives and lax.ppermute only.
A program may use at most 128 MiB of HBM per device.

v0:
```python
import jax
import jax.numpy as jnp
from jax import lax
from jax.sharding import PartitionSpec as P

GROUPS = 32
WIN = 128


def from_behind(value, axis, steps):
    count = lax.axis_size(axis)
    pairs = [(source, (source + steps) % count) for source in range(count)]
    return lax.ppermute(value, axis, pairs)


def with_halo(cells, sides, width):
    for axis, dim in sides:
        count = lax.axis_size(axis)
        head = lax.slice_in_dim(cells, 0, width, axis=dim)
        tail = lax.slice_in_dim(cells, cells.shape[dim] - width, cells.shape[dim], axis=dim)
        cells = jnp.concatenate(
            [
                lax.ppermute(tail, axis, [(i, (i + 1) % count) for i in range(count)]),
                cells,
                lax.ppermute(head, axis, [((i + 1) % count, i) for i in range(count)]),
            ],
            axis=dim,
        )
    return cells


def sinusoid(timestep, chans):
    half = chans // 2
    freq = jnp.exp(
        -jnp.log(jnp.float32(10000.0)) * jnp.arange(half, dtype=jnp.float32) / jnp.float32(half)
    )
    angle = timestep[0].astype(jnp.float32) * freq
    return jnp.concatenate([jnp.cos(angle), jnp.sin(angle)])


def stack_taps(framed, width_cols, height_rows):
    chans = framed.shape[0]
    return jnp.stack(
        [
            framed[:, tap_b : tap_b + width_cols, tap_a : tap_a + height_rows].reshape(
                chans, width_cols * height_rows
            )
            for tap_a in range(3)
            for tap_b in range(3)
        ]
    )


def body(
    latent,
    row_offset,
    col_offset,
    timestep,
    w_in,
    norm_gain,
    norm_shift,
    w_conv,
    w_time1,
    w_time2,
    w_time3,
):
    lat_chans, width_cols, height_rows = latent.shape
    chans = w_in.shape[1]
    group_size = WIN // width_cols
    col_count = lax.axis_size("col")
    own_tile = latent.astype(jnp.bfloat16)
    below = from_behind(own_tile, "row", -1)
    strip = lax.dynamic_slice_in_dim(
        jnp.concatenate([own_tile, below], axis=2), row_offset[0], height_rows, 2
    )
    beside = from_behind(strip, "col", -1)
    joined = jnp.concatenate([strip, beside], axis=1)
    col_index = lax.axis_index("col")
    phase = (col_index + col_count - group_size // 2) % col_count
    first_edge = phase % group_size == 0
    last_edge = phase % group_size == group_size - 1
    place = jnp.arange(width_cols + 2)
    dropped = (place == 0) & first_edge | (place == width_cols + 1) & last_edge

    def window_edges(framed):
        kept = jnp.where(dropped[None, :, None], jnp.zeros_like(framed), framed)
        return jnp.pad(kept, ((0, 0), (0, 0), (1, 1)))

    moved = lax.dynamic_slice_in_dim(joined, col_offset[0], width_cols, 1)
    framed = with_halo(moved, (("col", 1),), 1)
    framed = window_edges(framed)
    feat = jnp.einsum(
        "koc,kcp->op",
        w_in,
        stack_taps(framed, width_cols, height_rows),
        preferred_element_type=jnp.float32,
    )
    grouped = feat.reshape(GROUPS, -1)
    windows_across = col_count // group_size
    selector = (jnp.arange(windows_across) == phase // group_size).astype(jnp.float32)

    def spread_slots(values):
        return selector[:, None] * values[None, :]

    def own_slot(summed):
        return jnp.sum(selector[:, None] * summed, axis=0)

    count = jnp.float32(grouped.shape[1] * group_size)
    mean = own_slot(lax.psum(spread_slots(jnp.sum(grouped, axis=1)), "col")) / count
    centred = grouped - mean[:, None]
    var = own_slot(lax.psum(spread_slots(jnp.sum(centred * centred, axis=1)), "col")) / count
    normed = ((grouped - mean[:, None]) / jnp.sqrt(var[:, None] + 1e-05)).reshape(chans, -1)
    normed = normed * norm_gain[:, None] + norm_shift[:, None]
    hidden = jax.nn.silu(normed).astype(jnp.bfloat16).reshape(chans, width_cols, height_rows)
    padded = window_edges(with_halo(hidden, (("col", 1),), 1))
    hidden_taps = stack_taps(padded, width_cols, height_rows)
    emb = sinusoid(timestep, chans)
    full_one, full_two, full_three = (
        lax.all_gather(w_time1, "col", axis=1, tiled=True),
        lax.all_gather(w_time2, "col", axis=0, tiled=True),
        lax.all_gather(w_time3, "col", axis=1, tiled=True),
    )
    first = jnp.dot(emb, full_one.astype(jnp.float32), precision=lax.Precision.HIGHEST)
    e_one = jax.nn.silu(first).astype(jnp.bfloat16)
    e_two = jnp.dot(e_one, full_two, preferred_element_type=jnp.float32)
    s_two = jax.nn.silu(e_two).astype(jnp.bfloat16)
    tvec = jnp.dot(s_two, full_three, preferred_element_type=jnp.float32)
    conv = jnp.einsum(
        "koc,kcp->op",
        lax.all_gather(w_conv, "col", axis=1, tiled=True),
        hidden_taps,
        preferred_element_type=jnp.float32,
    )
    result = conv + tvec[:, None]
    return result.astype(jnp.bfloat16).reshape(chans, width_cols, height_rows)


def solution(mesh):
    return jax.shard_map(
        body,
        mesh=mesh,
        in_specs=(
            P(None, "col", "row"),
            P(),
            P(),
            P(),
            P(),
            P(),
            P(),
            P(None, "col", None),
            P(None, "col"),
            P("col", None),
            P(None, "col"),
        ),
        out_specs=P(None, "col", "row"),
        check_vma=False,
    )
```

profile of v0, /device:TPU:1, one launch (start us, length us, event | category | flops | bytes accessed | tf_op | source)
XLA Modules:
  0.0 393.5 jit_solution(3424629925423350221)
XLA Ops:
  6.5 0.7 all-gather.6.cloned.1.call-update
  7.3 0.8 convert_element_type.36
  8.2 10.2 %collective-permute-start = (bf16[4,32,128]{2,1,0:T(8,128)(2,1)S(1)}, bf16[4,32,128]{2,1,0:T(8,128)(2,1)S(1)}, u32[]{:S(2)}, u32[]{:S(2)}) collective-permute-start(bf16[4,32,128]{2,1,0:T(8,128)(2,1)S(1)} %convert_element_type.36), channel_id=1, source_target_pairs={{0,224},{32,0},{64,32},{96,64},{128,96},{160,128},{192,160},{224,1... | collective-permute-start | bytes 98312 | tf_op jit(solution)/shard_map/ppermute | solution.py:13
  18.3 1.6 copy.45
  20.7 49.0 %all_gather.13 = bf16[320,1280]{0,1:T(8,128)(2,1)S(1)} all-gather(bf16[320,40]{0,1:T(8,128)(2,1)} %param.19), channel_id=1, replica_groups=mesh['row'=8,'col'=32] {'col'}, dimensions={1}, use_global_device_ids=true | all-gather | bytes 844800 | tf_op jit(solution)/shard_map/all_gather | solution.py:119
  69.8 49.1 %all-gather = bf16[32,10,1280]{2,1,0:T(8,128)(2,1)} all-gather(bf16[1,10,1280]{2,1,0:T(8,128)(2,1)} %bitcast.56), channel_id=1, replica_groups=mesh['row'=8,'col'=32] {'col'}, dimensions={0}, use_global_device_ids=true | all-gather | bytes 844800 | tf_op jit(solution)/shard_map/all_gather | solution.py:121
  118.9 0.9 convolution_reduce_fusion.1
  120.6 0.2 collective-permute-start.1
  121.5 2.5 collective-permute-done.1
  124.2 0.5 collective-permute-start.3
  124.7 0.6 collective-permute-done.2
  125.3 2.1 collective-permute-done.3
  127.8 1.0 stack.6
  128.8 3.2 fusion.19
  132.3 69.9 %psum.14 = f32[8,32]{1,0:T(8,128)S(1)} all-reduce(f32[8,32]{1,0:T(8,128)S(1)} %broadcast_multiply_fusion.1), channel_id=1, replica_groups=mesh['row'=8,'col'=32] {'col'}, use_global_device_ids=true, to_apply=%region_2.3 | all-reduce | flops 256 | bytes 2048 | tf_op jit(solution)/shard_map/psum | solution.py:109
  202.5 3.2 multiply_reduce_fusion
  206.0 73.0 %psum.15 = f32[8,32]{1,0:T(8,128)S(1)} all-reduce(f32[8,32]{1,0:T(8,128)S(1)} %broadcast_multiply_fusion), channel_id=1, replica_groups=mesh['row'=8,'col'=32] {'col'}, use_global_device_ids=true, to_apply=%region_6.7 | all-reduce | flops 256 | bytes 2048 | tf_op jit(solution)/shard_map/psum | solution.py:111
  279.3 4.0 %fusion.6 = bf16[40,8,32,128]{3,1,2,0:T(8,128)(2,1)S(1)} fusion(f32[320]{0:T(512)S(1)} %copy-done.9, f32[320]{0:T(512)S(1)} %copy-done.10, f32[320]{0:T(512)S(1)} %div.51, f32[4096,320]{0,1:T(8,128)} %get-tuple-element.28, f32[320]{0:T(512)S(1)} %sub.29), kind=kLoop, calls=%fused_computation.18 | loop fusion | flops 11796480 | bytes 7869440
  283.3 0.6 copy.47
  283.9 1.0 fusion.17
  284.9 0.5 collective-permute-start.5
  285.5 1.4 reshape.46
  286.9 0.6 collective-permute-done.4
  287.5 2.5 collective-permute-done.5
  290.0 3.2 maximum_select_fusion
  293.1 9.8 %pad_slice_fusion = (bf16[320,32,128]{2,1,0:T(8,128)(2,1)S(1)}, bf16[320,32,128]{2,1,0:T(8,128)(2,1)}, bf16[320,32,128]{2,1,0:T(8,128)(2,1)}, bf16[320,32,128]{2...) fusion(bf16[320,34,128]{2,1,0:T(8,128)(2,1)S(1)} %maximum_selec, ...), kind=kLoop, calls=%fused_computation | loop fusion | bytes 34734080 | tf_op jit(solution)/shard_map/slice | solution.py:45
  303.0 5.2 %stack_reshape.63 = bf16[1,320,4096]{2,1,0:T(8,128)(2,1)} reshape(bf16[320,32,128]{2,1,0:T(8,128)(2,1)} %get-tuple-element.13) | data formatting | bytes 5242880 | tf_op jit(solution)/shard_map/stack;reshape | solution.py:43
  308.1 3.5 constant_dynamic-update-slice_fusion.8
  311.7 5.2 %stack_reshape.64 = bf16[1,320,4096]{2,1,0:T(8,128)(2,1)} reshape(bf16[320,32,128]{2,1,0:T(8,128)(2,1)} %get-tuple-element.6) | data formatting | bytes 5242880 | tf_op jit(solution)/shard_map/stack;reshape | solution.py:43
  316.9 5.2 %stack_reshape.65 = bf16[1,320,4096]{2,1,0:T(8,128)(2,1)} reshape(bf16[320,32,128]{2,1,0:T(8,128)(2,1)} %get-tuple-element.7) | data formatting | bytes 5242880 | tf_op jit(solution)/shard_map/stack;reshape | solution.py:43
  322.0 5.2 %stack_reshape.66 = bf16[1,320,4096]{2,1,0:T(8,128)(2,1)} reshape(bf16[320,32,128]{2,1,0:T(8,128)(2,1)} %get-tuple-element.12) | data formatting | bytes 5242880 | tf_op jit(solution)/shard_map/stack;reshape | solution.py:43
  327.2 5.2 %stack_reshape.67 = bf16[1,320,4096]{2,1,0:T(8,128)(2,1)} reshape(bf16[320,32,128]{2,1,0:T(8,128)(2,1)} %get-tuple-element.11) | data formatting | bytes 5242880 | tf_op jit(solution)/shard_map/stack;reshape | solution.py:43
  332.4 5.2 %stack_reshape.68 = bf16[1,320,4096]{2,1,0:T(8,128)(2,1)} reshape(bf16[320,32,128]{2,1,0:T(8,128)(2,1)} %get-tuple-element.10) | data formatting | bytes 5242880 | tf_op jit(solution)/shard_map/stack;reshape | solution.py:43
  337.6 5.2 %stack_reshape.69 = bf16[1,320,4096]{2,1,0:T(8,128)(2,1)} reshape(bf16[320,32,128]{2,1,0:T(8,128)(2,1)} %get-tuple-element.8) | data formatting | bytes 5242880 | tf_op jit(solution)/shard_map/stack;reshape | solution.py:43
  342.8 5.2 %stack_reshape.70 = bf16[1,320,4096]{2,1,0:T(8,128)(2,1)} reshape(bf16[320,32,128]{2,1,0:T(8,128)(2,1)} %get-tuple-element.9) | data formatting | bytes 5242880 | tf_op jit(solution)/shard_map/stack;reshape | solution.py:43
  348.0 3.1 stack_reshape.71
  351.0 3.7 constant_dynamic-update-slice_fusion.7
  354.8 1.8 constant_dynamic-update-slice_fusion.6
  356.6 1.9 constant_dynamic-update-slice_fusion.5
  358.4 1.8 constant_dynamic-update-slice_fusion.4
  360.3 1.8 constant_dynamic-update-slice_fusion.3
  362.0 1.8 constant_dynamic-update-slice_fusion.2
  363.8 1.7 constant_dynamic-update-slice_fusion.1
  365.5 1.8 constant_dynamic-update-slice_fusion
  367.4 2.5 convolution_reduce_fusion
  369.9 0.3 convolution_reduce_fusion.2
  370.3 14.3 %fusion.8 = bf16[40,8,32,128]{3,1,2,0:T(8,128)(2,1)S(1)} fusion(f32[320]{0:T(512)S(1)} %convolution_reduce_fusion.2, bf16[9,320,4096]{2,1,0:T(8,128)(2,1)} %constant_dynamic-update-slice_fusion, bf16[9,320,320]{2,0,1:T(8,128)(2,1)} %all-gather.4.cloned.1.call-done), kind=kOutput, calls=%fused_computation.20 | convolution fusion | flops 7552368640 | bytes 28058880 | tf_op jit(solution)/shard_map/koc,kcp->op/dot_general | solution.py:128
  384.6 2.1 copy.48
  (67 shorter events, 2.0 us)
Async XLA Ops:
  6.5 122.3 %copy-start = (bf16[9,320,4]{1,2,0:T(4,128)(2,1)S(1)}, bf16[9,320,4]{1,2,0:T(4,128)(2,1)}, u32[]{:S(2)}) copy-start(bf16[9,320,4]{1,2,0:T(4,128)(2,1)} %param.15) | copy-start | bytes 69124
  6.5 360.8 %all-gather.6.cloned.1.call-start = ((), (), s32[]{:S(2)}) async-start(), calls=%async_computation.1 | async-start | bytes 3379200 | tf_op jit(solution)/shard_map/all_gather | solution.py:120
  7.3 363.0 %all-gather.4.cloned.1.call-start = ((), (), s32[]{:S(2)}) async-start(), calls=%async_computation | async-start | bytes 4055040 | tf_op jit(solution)/shard_map/all_gather | solution.py:130
  8.2 112.3 %collective-permute-start = (bf16[4,32,128]{2,1,0:T(8,128)(2,1)S(1)}, bf16[4,32,128]{2,1,0:T(8,128)(2,1)S(1)}, u32[]{:S(2)}, u32[]{:S(2)}) collective-permute-start(bf16[4,32,128]{2,1,0:T(8,128)(2,1)S(1)} %convert_element_type.36), channel_id=1, source_target_pairs={{0,224},{32,0},{64,32},{96,64},{128,96},{160,128},{192,160},{224,1... | collective-permute-start | bytes 98312 | tf_op jit(solution)/shard_map/ppermute | solution.py:13
  120.6 3.4 collective-permute-start.1
  124.1 1.2 collective-permute-start.2
  124.2 3.3 collective-permute-start.3
  128.8 150.5 %copy-start.9 = (f32[320]{0:T(512)S(1)}, f32[320]{0:T(512)}, u32[]{:S(2)}) copy-start(f32[320]{0:T(512)} %param.17) | copy-start | bytes 3844
  128.8 150.5 %copy-start.10 = (f32[320]{0:T(512)S(1)}, f32[320]{0:T(512)}, u32[]{:S(2)}) copy-start(f32[320]{0:T(512)} %param.16) | copy-start | bytes 3844
  284.9 2.6 collective-permute-start.4
  284.9 5.1 %collective-permute-start.5 = (bf16[320,1,128]{2,1,0:T(2,128)(2,1)}, bf16[320,1,128]{2,1,0:T(2,128)(2,1)}, u32[]{:S(2)}, u32[]{:S(2)}) collective-permute-start(bf16[320,1,128]{2,1,0:T(2,128)(2,1)} %get-tuple-element.15), channel_id=1, source_target_pairs={{1,0},{2,1},{3,2},{4,3},{5,4},{6,5},{7,6},{8,7},{9,8},{10,9},{11,1... | collective-permute-start | bytes 245768 | tf_op jit(solution)/shard_map/ppermute | solution.py:25
  351.0 3.7 copy-start.8
  351.0 5.5 %copy-start.7 = (bf16[1,320,4096]{2,1,0:T(8,128)(2,1)S(1)}, bf16[1,320,4096]{2,1,0:T(8,128)(2,1)}, u32[]{:S(2)}) copy-start(bf16[1,320,4096]{2,1,0:T(8,128)(2,1)} %stack_reshape.66) | copy-start | bytes 7864324
  354.8 3.7 copy-start.6
  356.6 3.7 copy-start.5
  358.4 3.6 copy-start.4
  360.2 3.5 copy-start.2
  362.0 3.5 copy-start.3
  370.3 16.4 %copy-start.1 = (bf16[9,320,4]{1,2,0:T(4,128)(2,1)S(1)}, bf16[9,320,4]{1,2,0:T(4,128)(2,1)}, u32[]{:S(2)}) copy-start(bf16[9,320,4]{1,2,0:T(4,128)(2,1)} %param.15) | copy-start | bytes 69124
Sparse Core Ops, SparseCore 0:
  9.2 67.9 all-gather.5
  79.1 63.8 all-gather.3
where the time goes:
time: 402 us; the launch traced here: 394 us
  blocking collectives  241 us (60%)
  local copies, waits for them, and re-layouts  82.8 us (21%)
  matrix products  21.2 us (5%)
  between operations  15.7 us (4%)
  other arithmetic  12.1 us (3%)
  starting transfers between devices  11.6 us (3%)
  waiting for transfers between devices  9.06 us (2%)
    psum x1, blocking collectives, body(): lax.psum(spread_slots(jnp.sum(centred * centred, axis=1)), 'col')  73 us
    psum x1, blocking collectives, body(): lax.psum(spread_slots(jnp.sum(grouped, axis=1)), 'col')  69.9 us
    all_gather x1, blocking collectives, body(): lax.all_gather(w_time3, 'col', axis=1, tiled=True)  49.1 us
    all_gather x1, blocking collectives, body(): lax.all_gather(w_time1, 'col', axis=1, tiled=True)  49 us
    another operation x20, local copies, waits for them, and re-layouts, stack_taps(): jnp.stack([framed[:, tap_b:tap_b + width_cols, tap_a:tap_a + height_rows]...  47.5 us
    unnamed x34, local copies, waits for them, and re-layouts  23.8 us
    dot_general x1, matrix products, body(): jnp.einsum('koc,kcp->op', lax.all_gather(w_conv, 'col', axis=1, tiled=Tru...  14.3 us
    ppermute x2, starting transfers between devices, from_behind(): return lax.ppermute(value, axis, pairs)  10.4 us
  transfers between devices with their start and end apart: 8, of which 5 were waited for; matrix products, arithmetic and copies ran while one was open for 25% of the time, Pallas kernels for 0%

commit v1 on v0

v1 whole, which is shorter than its diff:
```python
import jax
import jax.numpy as jnp
from jax import lax
from jax.experimental import pallas as pl
from jax.experimental.pallas import tpu as pltpu
from jax.sharding import PartitionSpec as P

WIN = 128
LANES = 128
EDGE = 2
HIGH = lax.Precision.HIGHEST
ROWS = 8
TAPS = 9


def features_kernel(phase_ref, window_ref, w_ref, gain_ref, shift_ref, hidden_ref, shifted):
    chans = w_ref.shape[0]
    tile = window_ref.shape[2]
    width = tile // LANES
    lat = window_ref.shape[1]
    span = WIN * LANES
    total = span + 2 * EDGE * LANES
    lane = lax.broadcasted_iota(jnp.int32, (ROWS, tile), 1) % LANES
    zeros_edge = jnp.zeros((ROWS, EDGE * LANES), jnp.float32)
    for a in range(3):
        shifted[a, :, 0 : EDGE * LANES] = zeros_edge
        shifted[a, :, total - EDGE * LANES : total] = zeros_edge
    for part in range(window_ref.shape[0]):
        cells = window_ref[part].astype(jnp.float32)
        cells = jnp.concatenate([cells, jnp.zeros((ROWS - lat, tile), jnp.float32)], axis=0)
        at = EDGE * LANES + part * tile
        shifted[0, :, at : at + tile] = jnp.where(lane == 0, 0.0, pltpu.roll(cells, 1, 1))
        shifted[1, :, at : at + tile] = cells
        shifted[2, :, at : at + tile] = jnp.where(
            lane == LANES - 1, 0.0, pltpu.roll(cells, tile - 1, 1)
        )

    def tap_views(start, size):
        return [
            shifted[a, :, pl.ds(start + (b - 1) * LANES, size)]
            for a in range(3)
            for b in range(3)
        ]

    count = float(span)
    sums = [jnp.sum(v, axis=1, keepdims=True) for v in tap_views(EDGE * LANES, span)]
    xbar = jnp.concatenate(sums, axis=0) * (1.0 / count)

    def gram_step(step, carry):
        same, cross = carry
        start = pl.multiple_of(EDGE * LANES + step * 2048, LANES)
        cells = jnp.concatenate(
            [
                shifted[a, :, pl.ds(pl.multiple_of(start + (b - 1) * LANES, LANES), 2048)]
                for a in range(3)
                for b in range(3)
            ],
            axis=0,
        )
        centred = cells - xbar
        high = centred.astype(jnp.bfloat16)
        low = (centred - high.astype(jnp.float32)).astype(jnp.bfloat16)
        dims = (((1,), (1,)), ((), ()))
        same = same + lax.dot_general(high, high, dims, preferred_element_type=jnp.float32)
        cross = cross + lax.dot_general(high, low, dims, preferred_element_type=jnp.float32)
        return same, cross

    depth = TAPS * ROWS
    blank = jnp.zeros((depth, depth), jnp.float32)
    same, cross = lax.fori_loop(0, span // 2048, gram_step, (blank, blank))
    spread = (same + 2.0 * cross) * (1.0 / count)
    w_bf = w_ref[...]
    w = w_bf.astype(jnp.float32)
    chan_mean = jnp.dot(
        w, jnp.broadcast_to(xbar, (depth, LANES)), precision=HIGH, preferred_element_type=jnp.float32
    )
    quad = jnp.dot(w, spread, precision=HIGH, preferred_element_type=jnp.float32) * w
    chan_var = jnp.sum(quad, axis=1, keepdims=True)
    of_row = (lax.broadcasted_iota(jnp.int32, (chans, chans), 0) * 6554) >> 16
    of_col = (lax.broadcasted_iota(jnp.int32, (chans, chans), 1) * 6554) >> 16
    member = (of_row == of_col).astype(jnp.float32)
    mean = jnp.dot(member, chan_mean, precision=HIGH, preferred_element_type=jnp.float32) * 0.1
    off = chan_mean - mean
    var = jnp.dot(member, chan_var + off * off, precision=HIGH, preferred_element_type=jnp.float32) * 0.1
    scale = 0.5 * gain_ref[...] / jnp.sqrt(var + 1e-05)
    base = 0.5 * shift_ref[...] - mean * scale

    phase = phase_ref[0]
    first, last = phase == 0, phase == 3
    scale2 = jnp.concatenate([scale, scale], axis=1)
    base2 = jnp.concatenate([base, base], axis=1)
    pairs = (width + 2) // 2
    for pair in range(pairs):
        start = phase * tile + pair * 2 * LANES
        cells = jnp.concatenate(
            [
                shifted[a, :, pl.ds(pl.multiple_of(start + b * LANES, LANES), 2 * LANES)]
                for a in range(3)
                for b in range(3)
            ],
            axis=0,
        ).astype(jnp.bfloat16)
        feat = jnp.dot(w_bf, cells, preferred_element_type=jnp.float32)
        half = feat * scale2 + base2
        act = half * jnp.tanh(half) + half
        if pair == 0:
            keep = jnp.where(first, 0.0, 1.0)
            act = jnp.concatenate([jnp.where(first, 0.0, act[:, :LANES]), act[:, LANES:]], axis=1)
        if pair == pairs - 1:
            act = jnp.concatenate([act[:, :LANES], jnp.where(last, 0.0, act[:, LANES:])], axis=1)
        hidden_ref[:, pair * 2 * LANES : (pair + 1) * 2 * LANES] = act.astype(jnp.bfloat16)


def features(phase, window, w_taps, gain, shift):
    parts, lat, tile = window.shape
    chans = w_taps.shape[0]
    width = tile // LANES
    return pl.pallas_call(
        features_kernel,
        out_shape=jax.ShapeDtypeStruct((chans, (width + 2) * LANES), jnp.bfloat16),
        in_specs=[pl.BlockSpec(memory_space=pltpu.SMEM)]
        + [pl.BlockSpec(memory_space=pltpu.VMEM)] * 4,
        out_specs=pl.BlockSpec(memory_space=pltpu.VMEM),
        scratch_shapes=[pltpu.VMEM((3, ROWS, (WIN + 2 * EDGE) * LANES), jnp.float32)],
        compiler_params=pltpu.CompilerParams(vmem_limit_bytes=40 * 2**20),
        name="features",
    )(phase, window, w_taps, gain, shift)


COLS = 4
HALF_COLS = 16
KPAD = 512


def conv_kernel(place_ref, hidden_ref, s2_ref, *rest):
    blocks = rest[:8]
    out_ref, wide = rest[8], rest[9]
    core, xpos = place_ref[0], place_ref[1]
    step = pl.program_id(0)
    chans = hidden_ref.shape[0]
    half = chans // 2
    own = pl.multiple_of(core * half, 16)
    other = pl.multiple_of((1 - core) * half, 16)
    n = COLS * LANES
    lane = lax.broadcasted_iota(jnp.int32, (80, n), 1) % LANES
    tvecs = []
    for k in range(4):
        t_own = blocks[k][0:80, 3 * KPAD :].astype(jnp.float32) * s2_ref[0:1, :]
        t_oth = blocks[4 + k][0:80, 3 * KPAD :].astype(jnp.float32) * s2_ref[1:2, :]
        tvecs.append(jnp.sum(t_own + t_oth, axis=1, keepdims=True))

    def one(tile, _):
        col = step * HALF_COLS + tile * COLS
        right = []
        for rows in (own, other):
            for b in range(3):
                at = pl.multiple_of((col + b) * LANES, LANES)
                right.append(hidden_ref[pl.ds(rows, half), pl.ds(at, n)])
            right.append(right[-1][0 : KPAD - 3 * half])
        right = jnp.concatenate(right, axis=0)
        left = jnp.concatenate(
            [
                jnp.concatenate(
                    [
                        blocks[k][0:80, a * KPAD : (a + 1) * KPAD],
                        blocks[4 + k][0:80, a * KPAD : (a + 1) * KPAD],
                    ],
                    axis=1,
                )
                for k in range(4)
                for a in range(3)
            ],
            axis=0,
        )
        prod = jnp.dot(left, right, preferred_element_type=jnp.float32)
        for k in range(4):
            low, mid, high = (prod[(3 * k + a) * 80 : (3 * k + a + 1) * 80] for a in range(3))
            done = (
                mid
                + jnp.where(lane == 0, 0.0, pltpu.roll(low, 1, 1))
                + jnp.where(lane == LANES - 1, 0.0, pltpu.roll(high, n - 1, 1))
                + tvecs[k]
            )
            chan = (xpos + (0, 1, 3, 2)[k]) % 4 * 80
            for j in range(COLS):
                first = chan * HALF_COLS + tile * COLS + j
                wide[pl.ds(first, 80, stride=HALF_COLS), :] = done[:, j * LANES : (j + 1) * LANES]
        return 0

    lax.fori_loop(0, HALF_COLS // COLS, one, 0)
    out_ref[...] = wide[...].reshape(chans, HALF_COLS, LANES).astype(jnp.bfloat16)


def conv(place, hidden, s_two, blocks):
    chans, padded = hidden.shape
    width = padded // LANES - 2
    whole = lambda *shape: pl.BlockSpec(shape, lambda i: (0,) * len(shape))
    return pl.pallas_call(
        conv_kernel,
        grid=(width // HALF_COLS,),
        out_shape=jax.ShapeDtypeStruct((chans, width, LANES), jnp.bfloat16),
        in_specs=[
            pl.BlockSpec(memory_space=pltpu.SMEM),
            whole(*hidden.shape),
            whole(*s_two.shape),
        ]
        + [whole(*b.shape) for b in blocks],
        out_specs=pl.BlockSpec((chans, HALF_COLS, LANES), lambda i: (0, i, 0)),
        scratch_shapes=[pltpu.VMEM((chans * HALF_COLS, LANES), jnp.float32)],
        compiler_params=pltpu.CompilerParams(vmem_limit_bytes=56 * 2**20),
        name="convolve",
    )(place, hidden, s_two, *blocks)


def pairs_of(move):
    pairs = []
    for row in range(8):
        for col in range(32):
            y, z_hi, x, z_lo, core = row // 2, row % 2, col // 8, col // 2 % 4, col % 2
            z = z_hi * 4 + z_lo
            y, z, x, core = move(y, z, x, core)
            y, z, x = y % 4, z % 8, x % 4
            pairs.append((row * 32 + col, (y * 2 + z // 4) * 32 + x * 8 + z % 4 * 2 + core))
    return pairs


def send(value, move):
    return lax.ppermute(value, ("row", "col"), pairs_of(move))


def fetch_grid(value, rows, cols):
    pairs = [
        ((r + rows) % 8 * 32 + (c + cols) % 32, r * 32 + c) for r in range(8) for c in range(32)
    ]
    return lax.ppermute(value, ("row", "col"), pairs)


def swap_core(value):
    return send(value, lambda y, z, x, core: (y, z, x, 1 - core))


def from_z(value, steps):
    return send(value, lambda y, z, x, core: (y, z - steps, x, core))


def from_x(value, steps):
    return send(value, lambda y, z, x, core: (y, z, x - steps, core))


WINDOW_GROUPS = [[r * 32 + (4 * p + 2 + k) % 32 for k in range(4)] for r in range(8) for p in range(8)]


def sinusoid(timestep, chans):
    half = chans // 2
    freq = jnp.exp(
        -jnp.log(jnp.float32(10000.0)) * jnp.arange(half, dtype=jnp.float32) / jnp.float32(half)
    )
    angle = timestep[0].astype(jnp.float32) * freq
    return jnp.concatenate([jnp.cos(angle), jnp.sin(angle)])


def split_rows(value, width, rows):
    high = lax.reduce_precision(value, 8, 7)
    low = lax.reduce_precision(value - high, 8, 7)
    both = jnp.stack([high, low]).astype(jnp.bfloat16)
    return jnp.pad(both, ((0, rows - 2), (0, width - value.shape[0])))


def join_rows(rows, size):
    rows = rows[:, :size].astype(jnp.float32)
    return rows[0] + rows[1]


def body(
    latent,
    row_offset,
    col_offset,
    timestep,
    w_in,
    norm_gain,
    norm_shift,
    w_conv,
    w_time1,
    w_time2,
    w_time3,
):
    chans, lat = w_in.shape[1:]
    width, height = latent.shape[1:]
    temb = w_time2.shape[1]
    shard = w_conv.shape[1]
    col = lax.axis_index("col")
    core, z_lo, x = col % 2, col // 2 % 4, col // 8
    phase = (col + 30) % 4

    own = latent.astype(jnp.bfloat16)
    below, beside, corner = fetch_grid(own, 1, 0), fetch_grid(own, 0, 1), fetch_grid(own, 1, 1)

    emb = sinusoid(timestep, chans)
    first = jnp.dot(emb, w_time1.astype(jnp.float32), precision=lax.Precision.HIGHEST)
    e_one = jax.nn.silu(first).astype(jnp.bfloat16)
    e_two = jnp.dot(e_one, w_time2, preferred_element_type=jnp.float32)

    taps = w_conv.reshape(3, 3, shard, 2, chans // 2).transpose(3, 2, 0, 1, 4)
    taps = taps.reshape(2, shard, 3, 3 * (chans // 2))
    taps = jnp.pad(taps, ((0, 0), (0, 0), (0, 0), (0, KPAD - 3 * (chans // 2)))).reshape(2, shard, 3 * KPAD)
    third = w_time3.T.reshape(shard, 2, temb // 2).transpose(1, 0, 2)
    halves = jnp.concatenate([taps, third], axis=2)
    wide = halves.shape[2]
    mine = lax.dynamic_index_in_dim(halves, core, 0, keepdims=False)
    theirs = lax.dynamic_index_in_dim(halves, 1 - core, 0, keepdims=False)
    got = swap_core(jnp.concatenate([theirs, split_rows(e_two, wide, 2)]))
    e_two = e_two + join_rows(got[shard:], temb)
    pair = jnp.where(
        core == 0,
        jnp.concatenate([mine, got[:shard]]),
        jnp.concatenate([got[:shard], mine]),
    )
    zrow = jnp.concatenate([pair, split_rows(e_two, wide, 2)])
    near = [zrow, from_z(zrow, 1), from_z(zrow, 2), from_z(zrow, -1)]
    e_two = sum([join_rows(v[2 * shard :], temb) for v in near[1:]], e_two)
    ring = jnp.concatenate([v[: 2 * shard] for v in near + near])
    block = lax.dynamic_slice_in_dim(ring, (4 - z_lo) % 4 * 2 * shard, 8 * shard, 0)
    block = jnp.concatenate([block, split_rows(e_two, wide, 8)])
    after, before = from_x(block, 1), from_x(block, -1)
    cut = 48
    across = jnp.concatenate([from_x(after[:cut], 1), from_x(before[cut:], -1)])
    blocks = [block, after, before, across]
    e_two = sum([join_rows(v[8 * shard : 8 * shard + 2], temb) for v in blocks[1:]], e_two)
    blocks = blocks + [swap_core(v) for v in blocks]
    s_two = jax.nn.silu(e_two).astype(jnp.bfloat16).astype(jnp.float32).reshape(2, temb // 2)
    s_two = jnp.where(core == 0, s_two, s_two[::-1])

    grid = jnp.concatenate(
        [jnp.concatenate([own, below], axis=2), jnp.concatenate([beside, corner], axis=2)], axis=1
    )
    moved = lax.dynamic_slice(grid, (0, col_offset[0], row_offset[0]), (lat, width, height))
    window = lax.all_gather(
        moved.reshape(lat, width * height), ("row", "col"), axis_index_groups=WINDOW_GROUPS, axis=0
    )
    w_taps = jnp.pad(w_in.transpose(1, 0, 2), ((0, 0), (0, 0), (0, ROWS - lat))).reshape(chans, TAPS * ROWS)
    wide_gain = jnp.broadcast_to(norm_gain[:, None], (chans, LANES))
    wide_shift = jnp.broadcast_to(norm_shift[:, None], (chans, LANES))
    hidden = features(phase[None], window, w_taps, wide_gain, wide_shift)
    return conv(jnp.stack([core, x]), hidden, s_two, blocks)


def solution(mesh):
    return jax.shard_map(
        body,
        mesh=mesh,
        in_specs=(
            P(None, "col", "row"),
            P(),
            P(),
            P(),
            P(),
            P(),
            P(),
            P(None, "col", None),
            P(None, "col"),
            P("col", None),
            P(None, "col"),
        ),
        out_specs=P(None, "col", "row"),
        check_vma=False,
    )
```

time: 402 us -> 84.7 us (0.21); the launches traced: 394 us -> 84.3 us
  blocking collectives: 241 us -> 12.1 us
  local copies, waits for them, and re-layouts: 82.8 us -> 6.73 us
  Pallas kernels: 0 us -> 22.7 us
  matrix products: 21.2 us -> 1.06 us
  starting transfers between devices: 11.6 us -> 26.2 us
  between operations: 15.7 us -> 2.53 us
  other arithmetic: 12.1 us -> 3.05 us
    psum x2 -> x0, blocking collectives: 143 us -> none  [the longest x1 73 us: body(): lax.psum(spread_slots(jnp.sum(centred * centred, axis=1)), 'col')]
    all_gather x2 -> x1, blocking collectives: 98.1 us -> 12.1 us  [body(): lax.all_gather(moved.reshape(lat, width * height), ('row', 'col'), axis_i...]
    another operation x20 -> x7, local copies, waits for them, and re-layouts: 47.5 us -> 0.05 us  [the longest x6 0.03 us: split_rows(): both = jnp.stack([high, low]).astype(jnp.bfloat16)]
    pallas_call x0 -> x2, Pallas kernels: none -> 22.7 us  [the longest x1 15.9 us: conv(): pl.pallas_call(conv_kernel, grid=(width // HALF_COLS,), out_shape=jax.Sha...]
    unnamed x34 -> x29, local copies, waits for them, and re-layouts: 23.8 us -> 2.85 us
    dot_general x5 -> x2, matrix products: 21.2 us -> 1.06 us  [the longest x1 0.88 us: body(): jnp.dot(emb, w_time1.astype(jnp.float32), precision=lax.Precision.HIGHEST)]
    ppermute x6 -> x15, starting transfers between devices: 11.6 us -> 26.2 us  [the longest x12 13.4 us: send(): return lax.ppermute(value, ('row', 'col'), pairs_of(move))]
    slice x4 -> x2, local copies, waits for them, and re-layouts: 11 us -> 0.03 us  [body(): across = jnp.concatenate([from_x(after[:cut], 1), from_x(before[cut:], -1)])]
  transfers between devices with their start and end apart: 8 -> 15, of which waited for: 5 -> 4; matrix products, arithmetic and copies ran while one was open for 25% -> 5% of each run, Pallas kernels for 0% -> 8%
where the time goes in v1:
time: 84.7 us; the launch traced here: 84.3 us
  starting transfers between devices  26.2 us (31%)
  Pallas kernels  22.7 us (27%)
  blocking collectives  12.1 us (14%)
  waiting for transfers between devices  9.85 us (12%)
  local copies, waits for them, and re-layouts  6.73 us (8%)
  other arithmetic  3.05 us (4%)
  between operations  2.53 us (3%)
  matrix products  1.06 us (1%)
    pallas_call x1, Pallas kernels, conv(): pl.pallas_call(conv_kernel, grid=(width // HALF_COLS,), out_shape=jax.Sha...  15.9 us
    ppermute x12, starting transfers between devices, send(): return lax.ppermute(value, ('row', 'col'), pairs_of(move))  13.4 us
    ppermute x3, starting transfers between devices, fetch_grid(): return lax.ppermute(value, ('row', 'col'), pairs)  12.9 us
    all_gather x1, blocking collectives, body(): lax.all_gather(moved.reshape(lat, width * height), ('row', 'col'), axis_i...  12.1 us
    ppermute x12, waiting for transfers between devices, send(): return lax.ppermute(value, ('row', 'col'), pairs_of(move))  9.84 us
    pallas_call x1, Pallas kernels, features(): pl.pallas_call(features_kernel, out_shape=jax.ShapeDtypeStruct((chans, (w...  6.8 us
    unnamed x29, local copies, waits for them, and re-layouts  2.85 us
  transfers between devices with their start and end apart: 15, of which 4 were waited for; matrix products, arithmetic and copies ran while one was open for 5% of the time, Pallas kernels for 8%

profile of v1, /device:TPU:1, one launch (start us, length us, event | category | flops | bytes accessed | tf_op | source)
XLA Modules:
  0.0 84.3 jit_solution(4956316294984068007)
XLA Ops:
  0.7 0.1 pad_maximum_fusion.3
  0.8 0.9 %convolution_bitcast_fusion = f32[40]{0:T(128)S(1)} fusion(f32[320,1]{0,1:T(1,128)S(1)} %reshape.40, bf16[320,40]{0,1:T(8,128)(2,1)} %param.19), kind=kOutput, calls=%fused_computation.1 | convolution fusion | flops 153600 | bytes 27040 | tf_op jit(solution)/shard_map/dot_general | solution.py:299
  1.7 0.2 convolution_reduce_fusion
  1.9 0.0 copy-start.10
  1.9 0.8 reshape.35
  2.8 1.0 %reshape.32 = bf16[3,3,10,2,160]{4,3,2,1,0:T(2,128)(2,1)S(1)} reshape(bf16[9,10,320]{2,1,0:T(8,128)(2,1)} %param.18) | data formatting | bytes 115200 | tf_op jit(solution)/shard_map/reshape | solution.py:303
  3.8 0.1 reshape.33
  4.0 0.0 copy-start.11
  4.0 0.1 pad.20
  4.1 0.2 dynamic-slice_maximum_fusion
  4.4 3.3 %collective-permute-start.3 = (bf16[12,2176]{1,0:T(8,128)(2,1)S(1)}, bf16[12,2176]{1,0:T(8,128)(2,1)S(1)}, u32[]{:S(2)}, u32[]{:S(2)}) collective-permute-start(bf16[12,2176]{1,0:T(8,128)(2,1)S(1)} %pad_maximum_fusion.2), channel_id=1, source_target_pairs={{0,1},{1,0},{2,3},{3,2},{4,5},{5,4},{6,7},{7,6},{8,9},{9,8},{10,11... | collective-permute-start | bytes 156680 | tf_op jit(solution)/shard_map/ppermute | solution.py:228
  7.8 0.9 %collective-permute-done.3 = bf16[12,2176]{1,0:T(8,128)(2,1)S(1)} collective-permute-done((bf16[12,2176]{1,0:T(8,128)(2,1)S(1)}, bf16[12,2176]{1,0:T(8,128)(2,1)S(1)}, u32[]{:S(2)}, u32[]{:S(2)}) %collective-permute-start.3) | collective-permute-done | bytes 52256 | tf_op jit(solution)/shard_map/ppermute | solution.py:228
  8.8 0.1 maximum_select_fusion
  8.9 0.1 collective-permute-start.6
  8.9 0.8 %convert_element_type.50 = bf16[4,32,128]{2,1,0:T(8,128)(2,1)S(1)} convert(f32[4,32,128]{2,1,0:T(8,128)} %param.11) | non-fusion elementwise | flops 16384 | bytes 98304 | tf_op jit(solution)/shard_map/convert_element_type | solution.py:295
  9.8 8.9 %collective-permute-start.2 = (bf16[4,32,128]{2,1,0:T(8,128)(2,1)S(1)}, bf16[4,32,128]{2,1,0:T(8,128)(2,1)S(1)}, u32[]{:S(2)}, u32[]{:S(2)}) collective-permute-start(bf16[4,32,128]{2,1,0:T(8,128)(2,1)S(1)} %convert_element_type.50), channel_id=1, source_target_pairs={{33,0},{34,1},{35,2},{36,3},{37,4},{38,5},{39,6},{40,7},{41,8},{42... | collective-permute-start | bytes 98312 | tf_op jit(solution)/shard_map/ppermute | solution.py:235
  18.7 0.0 collective-permute-start.1
  18.7 4.0 %collective-permute-start = (bf16[4,32,128]{2,1,0:T(8,128)(2,1)S(1)}, bf16[4,32,128]{2,1,0:T(8,128)(2,1)S(1)}, u32[]{:S(2)}, u32[]{:S(2)}) collective-permute-start(bf16[4,32,128]{2,1,0:T(8,128)(2,1)S(1)} %convert_element_type.50), channel_id=1, source_target_pairs={{32,0},{33,1},{34,2},{35,3},{36,4},{37,5},{38,6},{39,7},{40,8},{41... | collective-permute-start | bytes 98312 | tf_op jit(solution)/shard_map/ppermute | solution.py:235
  22.7 0.5 collective-permute-start.5
  23.2 0.7 collective-permute-start.4
  23.9 5.4 %collective-permute-done.5 = bf16[22,2176]{1,0:T(8,128)(2,1)S(1)} collective-permute-done((bf16[22,2176]{1,0:T(8,128)(2,1)S(1)}, bf16[22,2176]{1,0:T(8,128)(2,1)S(1)}, u32[]{:S(2)}, u32[]{:S(2)}) %collective-permute-start.5) | collective-permute-done | bytes 95776 | tf_op jit(solution)/shard_map/ppermute | solution.py:228
  29.5 1.1 %concatenate.45 = bf16[160,2176]{1,0:T(8,128)(2,1)S(1)} concatenate(bf16[20,2176]{1,0:T(8,128)(2,1)S(1)} %maximum_select_fusion, bf16[20,2176]{1,0:T(8,128)(2,1)S(1)} %bitcast.46, bf16[20,2176]{1,0:T(8,128)(2,1)S(1)} %bitcast.44, bf16[20,2176]{1,0:T(8,128)(2,1)S(1)} %bitcast.42, bf16[20,2176]{1,0:T(8,128)(2,1)S(1)} %maximum_select_fusion, bf16[20,2176]{1,0:T(8,128)(2,1)S(1)} %bitcast.47, ...), dimensions={0} | concatenate | bytes 1392640 | tf_op jit(solution)/shard_map/concatenate | solution.py:321
  30.6 0.1 constant_dynamic-slice_fusion
  30.8 2.2 %collective-permute-start.8 = (bf16[88,2176]{1,0:T(8,128)(2,1)S(1)}, bf16[88,2176]{1,0:T(8,128)(2,1)S(1)}, u32[]{:S(2)}, u32[]{:S(2)}) collective-permute-start(bf16[88,2176]{1,0:T(8,128)(2,1)S(1)} %pad_maximum_fusion.rest_0_), channel_id=1, source_target_pairs={{0,8},{1,9},{2,10},{3,11},{4,12},{5,13},{6,14},{7,15},{8,16},{9,17... | collective-permute-start | bytes 1148936 | tf_op jit(solution)/shard_map/ppermute | solution.py:228
  32.9 1.3 %collective-permute-start.7 = (bf16[88,2176]{1,0:T(8,128)(2,1)S(1)}, bf16[88,2176]{1,0:T(8,128)(2,1)S(1)}, u32[]{:S(2)}, u32[]{:S(2)}) collective-permute-start(bf16[88,2176]{1,0:T(8,128)(2,1)S(1)} %pad_maximum_fusion.rest_0_), channel_id=1, source_target_pairs={{0,24},{1,25},{2,26},{3,27},{4,28},{5,29},{6,30},{7,31},{8,0},{9,1... | collective-permute-start | bytes 1148936 | tf_op jit(solution)/shard_map/ppermute | solution.py:228
  34.2 0.6 pad_add_fusion.place_ref
  36.2 0.1 copy.18.w_ref
  36.3 0.2 fusion.7
  36.5 12.1 %all_gather.3.window_ref = bf16[4,4,4096]{2,1,0:T(4,128)(2,1)S(1)} all-gather(bf16[1,4,4096]{2,1,0:T(4,128)(2,1)S(1)} %all_gather_reshape.3), channel_id=1, replica_groups={{2,3,4,5},{6,7,8,9},{10,11,12,13},{14,15,16,17},{18,19,20,21},{22,23,24..., dimensions={0}, use_global_device_ids=true | all-gather | bytes 163840 | tf_op jit(solution)/shard_map/all_gather | solution.py:337
  48.6 0.1 broadcast_in_dim.7.gain_ref
  48.8 0.1 broadcast_in_dim.8.shift_ref
  48.9 6.8 %features.1.hidden_ref = bf16[320,4352]{1,0:T(8,128)(2,1)S(1)} custom-call(s32[1]{0:T(128)} %bitcast.2.phase_ref, bf16[4,4,4096]{2,1,0:T(4,128)(2,1)S(1)} %all_gather.3.window_ref, bf16[320,72]{1,0:T(8,128)(2,1)S(1)} %copy.18.w_ref, f32[320,128]{1,0:T(8,128)S(1)} %broadcast_in_dim.7.gain_ref, f32[320,128]{1,0:T(8,128)S(1)} %broadcast_in_dim.8.shift_ref), custom_call_target="tpu_custom_call" | custom-call | tf_op jit(solution)/shard_map/features/pallas_call | solution.py:118
  55.7 1.5 %copy-done.1 = bf16[320,4352]{1,0:T(8,128)(2,1)} copy-done((bf16[320,4352]{1,0:T(8,128)(2,1)}, bf16[320,4352]{1,0:T(8,128)(2,1)S(1)}, u32[]{:S(2)}) %copy-start.1) | copy-done | bytes 2785304
  57.2 0.2 collective-permute-start.11
  57.4 0.1 collective-permute-start.9
  57.5 2.7 %collective-permute-start.10 = (bf16[48,2176]{1,0:T(8,128)(2,1)S(1)}, bf16[48,2176]{1,0:T(8,128)(2,1)S(1)}, u32[]{:S(2)}, u32[]{:S(2)}) collective-permute-start(bf16[48,2176]{1,0:T(8,128)(2,1)S(1)} %slice.152), channel_id=1, source_target_pairs={{0,24},{1,25},{2,26},{3,27},{4,28},{5,29},{6,30},{7,31},{8,0},{9,1... | collective-permute-start | bytes 626696 | tf_op jit(solution)/shard_map/ppermute | solution.py:228
  60.3 0.9 %collective-permute-start.13 = (bf16[88,2176]{1,0:T(8,128)(2,1)S(1)}, bf16[88,2176]{1,0:T(8,128)(2,1)S(1)}, u32[]{:S(2)}, u32[]{:S(2)}) collective-permute-start(bf16[88,2176]{1,0:T(8,128)(2,1)S(1)} %collective-permute-done.8.rest_2_), channel_id=1, source_target_pairs={{0,1},{1,0},{2,3},{3,2},{4,5},{5,4},{6,7},{7,6},{8,9},{9,8},{10,11... | collective-permute-start | bytes 1148936 | tf_op jit(solution)/shard_map/ppermute | solution.py:228
  61.2 0.1 collective-permute-start.12
  61.3 3.0 %collective-permute-done.9 = bf16[40,2176]{1,0:T(8,128)(2,1)S(1)} collective-permute-done((bf16[40,2176]{1,0:T(8,128)(2,1)S(1)}, bf16[40,2176]{1,0:T(8,128)(2,1)S(1)}, u32[]{:S(2)}, u32[]{:S(2)}) %collective-permute-start.9) | collective-permute-done | bytes 174112 | tf_op jit(solution)/shard_map/ppermute | solution.py:228
  64.5 1.3 %collective-permute-start.14 = (bf16[88,2176]{1,0:T(8,128)(2,1)S(1)}, bf16[88,2176]{1,0:T(8,128)(2,1)S(1)}, u32[]{:S(2)}, u32[]{:S(2)}) collective-permute-start(bf16[88,2176]{1,0:T(8,128)(2,1)S(1)} %constant_dynamic-update-slice_fusion.rest_3_), channel_id=1, source_target_pairs={{0,1},{1,0},{2,3},{3,2},{4,5},{5,4},{6,7},{7,6},{8,9},{9,8},{10,11... | collective-permute-start | bytes 1148936 | tf_op jit(solution)/shard_map/ppermute | solution.py:228
  65.8 0.2 rev.3
  66.0 0.6 broadcast_select_fusion.s2_ref
  66.6 0.5 collective-permute-done.14.rest_7_
  67.1 0.2 copy-done.6
  67.3 0.1 copy-done.7
  67.5 0.2 copy-done.8
  67.6 0.7 copy-done.9
  68.4 15.9 %convolve.1 = bf16[320,32,128]{2,1,0:T(8,128)(2,1)} custom-call(s32[2]{0:T(128)} %pad_add_fusion.place_ref, bf16[320,4352]{1,0:T(8,128)(2,1)} %copy-done.1, f32[2,640]{1,0:T(2,128)} %broadcast_select_fusion.s2_ref, bf16[88,2176]{1,0:T(8,128)(2,1)} %copy-done.2, bf16[88,2176]{1,0:T(8,128)(2,1)} %copy-done.3, bf16[88,2176]{1,0:T(8,128)(2,1)} %copy-done.5, ...), custom_call_target="tpu_custom_call" | custom-call | tf_op jit(solution)/shard_map/convolve/pallas_call | solution.py:198
  (74 shorter events, 0.7 us)
Async XLA Ops:
  0.0 1.7 %copy-start = (bf16[40,1280]{1,0:T(8,128)(2,1)S(1)}, bf16[40,1280]{1,0:T(8,128)(2,1)}, u32[]{:S(2)}) copy-start(bf16[40,1280]{1,0:T(8,128)(2,1)} %param.20) | copy-start | bytes 307204
  1.9 32.3 %copy-start.10 = (bf16[9,320,4]{1,2,0:T(4,128)(2,1)S(1)}, bf16[9,320,4]{1,2,0:T(4,128)(2,1)}, u32[]{:S(2)}) copy-start(bf16[9,320,4]{1,2,0:T(4,128)(2,1)} %param.15) | copy-start | bytes 69124
  4.0 44.6 %copy-start.11 = (f32[320]{0:T(512)S(1)}, f32[320]{0:T(512)}, u32[]{:S(2)}) copy-start(f32[320]{0:T(512)} %param.16) | copy-start | bytes 3844
  4.1 44.7 %copy-start.12 = (f32[320]{0:T(512)S(1)}, f32[320]{0:T(512)}, u32[]{:S(2)}) copy-start(f32[320]{0:T(512)} %param.17) | copy-start | bytes 3844
  4.4 4.2 %collective-permute-start.3 = (bf16[12,2176]{1,0:T(8,128)(2,1)S(1)}, bf16[12,2176]{1,0:T(8,128)(2,1)S(1)}, u32[]{:S(2)}, u32[]{:S(2)}) collective-permute-start(bf16[12,2176]{1,0:T(8,128)(2,1)S(1)} %pad_maximum_fusion.2), channel_id=1, source_target_pairs={{0,1},{1,0},{2,3},{3,2},{4,5},{5,4},{6,7},{7,6},{8,9},{9,8},{10,11... | collective-permute-start | bytes 156680 | tf_op jit(solution)/shard_map/ppermute | solution.py:228
  8.9 14.3 %collective-permute-start.6 = (bf16[22,2176]{1,0:T(8,128)(2,1)S(1)}, bf16[22,2176]{1,0:T(8,128)(2,1)S(1)}, u32[]{:S(2)}, u32[]{:S(2)}) collective-permute-start(bf16[22,2176]{1,0:T(8,128)(2,1)S(1)} %pad_maximum_fusion.1), channel_id=1, source_target_pairs={{0,2},{1,3},{2,4},{3,5},{4,6},{5,7},{6,32},{7,33},{8,10},{9,11},{1... | collective-permute-start | bytes 287240 | tf_op jit(solution)/shard_map/ppermute | solution.py:228
  9.8 26.5 %collective-permute-start.2 = (bf16[4,32,128]{2,1,0:T(8,128)(2,1)S(1)}, bf16[4,32,128]{2,1,0:T(8,128)(2,1)S(1)}, u32[]{:S(2)}, u32[]{:S(2)}) collective-permute-start(bf16[4,32,128]{2,1,0:T(8,128)(2,1)S(1)} %convert_element_type.50), channel_id=1, source_target_pairs={{33,0},{34,1},{35,2},{36,3},{37,4},{38,5},{39,6},{40,7},{41,8},{42... | collective-permute-start | bytes 98312 | tf_op jit(solution)/shard_map/ppermute | solution.py:235
  18.7 17.6 %collective-permute-start.1 = (bf16[4,32,128]{2,1,0:T(8,128)(2,1)S(1)}, bf16[4,32,128]{2,1,0:T(8,128)(2,1)S(1)}, u32[]{:S(2)}, u32[]{:S(2)}) collective-permute-start(bf16[4,32,128]{2,1,0:T(8,128)(2,1)S(1)} %convert_element_type.50), channel_id=1, source_target_pairs={{1,0},{2,1},{3,2},{4,3},{5,4},{6,5},{7,6},{8,7},{9,8},{10,9},{11,1... | collective-permute-start | bytes 98312 | tf_op jit(solution)/shard_map/ppermute | solution.py:235
  18.7 17.6 %collective-permute-start = (bf16[4,32,128]{2,1,0:T(8,128)(2,1)S(1)}, bf16[4,32,128]{2,1,0:T(8,128)(2,1)S(1)}, u32[]{:S(2)}, u32[]{:S(2)}) collective-permute-start(bf16[4,32,128]{2,1,0:T(8,128)(2,1)S(1)} %convert_element_type.50), channel_id=1, source_target_pairs={{32,0},{33,1},{34,2},{35,3},{36,4},{37,5},{38,6},{39,7},{40,8},{41... | collective-permute-start | bytes 98312 | tf_op jit(solution)/shard_map/ppermute | solution.py:235
  22.7 6.7 %collective-permute-start.5 = (bf16[22,2176]{1,0:T(8,128)(2,1)S(1)}, bf16[22,2176]{1,0:T(8,128)(2,1)S(1)}, u32[]{:S(2)}, u32[]{:S(2)}) collective-permute-start(bf16[22,2176]{1,0:T(8,128)(2,1)S(1)} %pad_maximum_fusion.1), channel_id=1, source_target_pairs={{0,36},{1,37},{2,38},{3,39},{4,0},{5,1},{6,2},{7,3},{8,44},{9,45},... | collective-permute-start | bytes 287240 | tf_op jit(solution)/shard_map/ppermute | solution.py:228
  23.2 6.2 %collective-permute-start.4 = (bf16[22,2176]{1,0:T(8,128)(2,1)S(1)}, bf16[22,2176]{1,0:T(8,128)(2,1)S(1)}, u32[]{:S(2)}, u32[]{:S(2)}) collective-permute-start(bf16[22,2176]{1,0:T(8,128)(2,1)S(1)} %pad_maximum_fusion.1), channel_id=1, source_target_pairs={{0,38},{1,39},{2,0},{3,1},{4,2},{5,3},{6,4},{7,5},{8,46},{9,47},{1... | collective-permute-start | bytes 287240 | tf_op jit(solution)/shard_map/ppermute | solution.py:228
  30.8 33.7 %copy-start.2 = (bf16[88,2176]{1,0:T(8,128)(2,1)}, bf16[88,2176]{1,0:T(8,128)(2,1)S(1)}, u32[]{:S(2)}) copy-start(bf16[88,2176]{1,0:T(8,128)(2,1)S(1)} %pad_maximum_fusion.rest_0_) | copy-start | bytes 1148932
  30.8 26.6 %collective-permute-start.8 = (bf16[88,2176]{1,0:T(8,128)(2,1)S(1)}, bf16[88,2176]{1,0:T(8,128)(2,1)S(1)}, u32[]{:S(2)}, u32[]{:S(2)}) collective-permute-start(bf16[88,2176]{1,0:T(8,128)(2,1)S(1)} %pad_maximum_fusion.rest_0_), channel_id=1, source_target_pairs={{0,8},{1,9},{2,10},{3,11},{4,12},{5,13},{6,14},{7,15},{8,16},{9,17... | collective-permute-start | bytes 1148936 | tf_op jit(solution)/shard_map/ppermute | solution.py:228
  32.9 24.5 %collective-permute-start.7 = (bf16[88,2176]{1,0:T(8,128)(2,1)S(1)}, bf16[88,2176]{1,0:T(8,128)(2,1)S(1)}, u32[]{:S(2)}, u32[]{:S(2)}) collective-permute-start(bf16[88,2176]{1,0:T(8,128)(2,1)S(1)} %pad_maximum_fusion.rest_0_), channel_id=1, source_target_pairs={{0,24},{1,25},{2,26},{3,27},{4,28},{5,29},{6,30},{7,31},{8,0},{9,1... | collective-permute-start | bytes 1148936 | tf_op jit(solution)/shard_map/ppermute | solution.py:228
  55.7 1.5 %copy-start.1 = (bf16[320,4352]{1,0:T(8,128)(2,1)}, bf16[320,4352]{1,0:T(8,128)(2,1)S(1)}, u32[]{:S(2)}) copy-start(bf16[320,4352]{1,0:T(8,128)(2,1)S(1)} %features.1.hidden_ref) | copy-start | bytes 8355844
  57.2 9.4 %collective-permute-start.11 = (bf16[88,2176]{1,0:T(8,128)(2,1)S(1)}, bf16[88,2176]{1,0:T(8,128)(2,1)S(1)}, u32[]{:S(2)}, u32[]{:S(2)}) collective-permute-start(bf16[88,2176]{1,0:T(8,128)(2,1)S(1)} %pad_maximum_fusion.rest_0_), channel_id=1, source_target_pairs={{0,1},{1,0},{2,3},{3,2},{4,5},{5,4},{6,7},{7,6},{8,9},{9,8},{10,11... | collective-permute-start | bytes 1148936 | tf_op jit(solution)/shard_map/ppermute | solution.py:228
  57.4 9.7 %copy-start.5 = (bf16[88,2176]{1,0:T(8,128)(2,1)}, bf16[88,2176]{1,0:T(8,128)(2,1)S(1)}, u32[]{:S(2)}) copy-start(bf16[88,2176]{1,0:T(8,128)(2,1)S(1)} %collective-permute-done.8.rest_2_) | copy-start | bytes 1148932
  57.4 6.9 %collective-permute-start.9 = (bf16[40,2176]{1,0:T(8,128)(2,1)S(1)}, bf16[40,2176]{1,0:T(8,128)(2,1)S(1)}, u32[]{:S(2)}, u32[]{:S(2)}) collective-permute-start(bf16[40,2176]{1,0:T(8,128)(2,1)S(1)} %slice.148), channel_id=1, source_target_pairs={{0,8},{1,9},{2,10},{3,11},{4,12},{5,13},{6,14},{7,15},{8,16},{9,17... | collective-permute-start | bytes 522248 | tf_op jit(solution)/shard_map/ppermute | solution.py:228
  57.5 9.6 %copy-start.3 = (bf16[88,2176]{1,0:T(8,128)(2,1)}, bf16[88,2176]{1,0:T(8,128)(2,1)S(1)}, u32[]{:S(2)}) copy-start(bf16[88,2176]{1,0:T(8,128)(2,1)S(1)} %collective-permute-done.7.rest_1_) | copy-start | bytes 1148932
  57.5 6.8 %collective-permute-start.10 = (bf16[48,2176]{1,0:T(8,128)(2,1)S(1)}, bf16[48,2176]{1,0:T(8,128)(2,1)S(1)}, u32[]{:S(2)}, u32[]{:S(2)}) collective-permute-start(bf16[48,2176]{1,0:T(8,128)(2,1)S(1)} %slice.152), channel_id=1, source_target_pairs={{0,24},{1,25},{2,26},{3,27},{4,28},{5,29},{6,30},{7,31},{8,0},{9,1... | collective-permute-start | bytes 626696 | tf_op jit(solution)/shard_map/ppermute | solution.py:228
  60.3 6.3 %collective-permute-start.13 = (bf16[88,2176]{1,0:T(8,128)(2,1)S(1)}, bf16[88,2176]{1,0:T(8,128)(2,1)S(1)}, u32[]{:S(2)}, u32[]{:S(2)}) collective-permute-start(bf16[88,2176]{1,0:T(8,128)(2,1)S(1)} %collective-permute-done.8.rest_2_), channel_id=1, source_target_pairs={{0,1},{1,0},{2,3},{3,2},{4,5},{5,4},{6,7},{7,6},{8,9},{9,8},{10,11... | collective-permute-start | bytes 1148936 | tf_op jit(solution)/shard_map/ppermute | solution.py:228
  61.2 5.4 %collective-permute-start.12 = (bf16[88,2176]{1,0:T(8,128)(2,1)S(1)}, bf16[88,2176]{1,0:T(8,128)(2,1)S(1)}, u32[]{:S(2)}, u32[]{:S(2)}) collective-permute-start(bf16[88,2176]{1,0:T(8,128)(2,1)S(1)} %collective-permute-done.7.rest_1_), channel_id=1, source_target_pairs={{0,1},{1,0},{2,3},{3,2},{4,5},{5,4},{6,7},{7,6},{8,9},{9,8},{10,11... | collective-permute-start | bytes 1148936 | tf_op jit(solution)/shard_map/ppermute | solution.py:228
  64.5 2.7 %copy-start.4 = (bf16[88,2176]{1,0:T(8,128)(2,1)}, bf16[88,2176]{1,0:T(8,128)(2,1)S(1)}, u32[]{:S(2)}) copy-start(bf16[88,2176]{1,0:T(8,128)(2,1)S(1)} %constant_dynamic-update-slice_fusion.rest_3_) | copy-start | bytes 1148932
  64.5 2.7 %collective-permute-start.14 = (bf16[88,2176]{1,0:T(8,128)(2,1)S(1)}, bf16[88,2176]{1,0:T(8,128)(2,1)S(1)}, u32[]{:S(2)}, u32[]{:S(2)}) collective-permute-start(bf16[88,2176]{1,0:T(8,128)(2,1)S(1)} %constant_dynamic-update-slice_fusion.rest_3_), channel_id=1, source_target_pairs={{0,1},{1,0},{2,3},{3,2},{4,5},{5,4},{6,7},{7,6},{8,9},{9,8},{10,11... | collective-permute-start | bytes 1148936 | tf_op jit(solution)/shard_map/ppermute | solution.py:228
  66.6 0.8 copy-start.6
  66.6 0.9 %copy-start.7 = (bf16[88,2176]{1,0:T(8,128)(2,1)}, bf16[88,2176]{1,0:T(8,128)(2,1)S(1)}, u32[]{:S(2)}) copy-start(bf16[88,2176]{1,0:T(8,128)(2,1)S(1)} %collective-permute-done.13.rest_6_) | copy-start | bytes 1148932
  66.6 1.0 %copy-start.8 = (bf16[88,2176]{1,0:T(8,128)(2,1)}, bf16[88,2176]{1,0:T(8,128)(2,1)S(1)}, u32[]{:S(2)}) copy-start(bf16[88,2176]{1,0:T(8,128)(2,1)S(1)} %collective-permute-done.12.rest_5_) | copy-start | bytes 1148932
  67.6 0.7 copy-start.9

commit v2 on v1

v2 whole, which is shorter than its diff:
```python
import jax
import jax.numpy as jnp
from jax import lax
from jax.experimental import pallas as pl
from jax.experimental.pallas import tpu as pltpu
from jax.sharding import PartitionSpec as P

WIN = 128
LANES = 128
EDGE = 2
HIGH = lax.Precision.HIGHEST
ROWS = 8
TAPS = 9


def features_kernel(phase_ref, window_ref, params_ref, hidden_ref, shifted):
    chans = hidden_ref.shape[0]
    tile = window_ref.shape[2]
    width = tile // LANES
    lat = window_ref.shape[1]
    span = WIN * LANES
    total = span + 2 * EDGE * LANES
    lane = lax.broadcasted_iota(jnp.int32, (ROWS, tile), 1) % LANES
    zeros_edge = jnp.zeros((ROWS, EDGE * LANES), jnp.float32)
    for a in range(3):
        shifted[a, :, 0 : EDGE * LANES] = zeros_edge
        shifted[a, :, total - EDGE * LANES : total] = zeros_edge
    for part in range(window_ref.shape[0]):
        cells = window_ref[part].astype(jnp.float32)
        cells = jnp.concatenate([cells, jnp.zeros((ROWS - lat, tile), jnp.float32)], axis=0)
        at = EDGE * LANES + part * tile
        shifted[0, :, at : at + tile] = jnp.where(lane == 0, 0.0, pltpu.roll(cells, 1, 1))
        shifted[1, :, at : at + tile] = cells
        shifted[2, :, at : at + tile] = jnp.where(
            lane == LANES - 1, 0.0, pltpu.roll(cells, tile - 1, 1)
        )

    def tap_views(start, size):
        return [
            shifted[a, :, pl.ds(start + (b - 1) * LANES, size)]
            for a in range(3)
            for b in range(3)
        ]

    depth = TAPS * ROWS
    columns = params_ref[...].T
    w = columns[0:chans, 0:depth]
    w_bf = w.astype(jnp.bfloat16)
    gain = jnp.broadcast_to(columns[0:chans, depth : depth + 1], (chans, LANES))
    shift = jnp.broadcast_to(columns[0:chans, depth + 1 : depth + 2], (chans, LANES))
    count = float(span)
    sums = [jnp.sum(v, axis=1, keepdims=True) for v in tap_views(EDGE * LANES, span)]
    xbar = jnp.concatenate(sums, axis=0) * (1.0 / count)

    def gram_step(step, carry):
        same, cross = carry
        start = pl.multiple_of(EDGE * LANES + step * 2048, LANES)
        cells = jnp.concatenate(
            [
                shifted[a, :, pl.ds(pl.multiple_of(start + (b - 1) * LANES, LANES), 2048)]
                for a in range(3)
                for b in range(3)
            ],
            axis=0,
        )
        centred = cells - xbar
        high = centred.astype(jnp.bfloat16)
        low = (centred - high.astype(jnp.float32)).astype(jnp.bfloat16)
        dims = (((1,), (1,)), ((), ()))
        same = same + lax.dot_general(high, high, dims, preferred_element_type=jnp.float32)
        cross = cross + lax.dot_general(high, low, dims, preferred_element_type=jnp.float32)
        return same, cross

    blank = jnp.zeros((depth, depth), jnp.float32)
    same, cross = lax.fori_loop(0, span // 2048, gram_step, (blank, blank))
    spread = (same + 2.0 * cross) * (1.0 / count)
    chan_mean = jnp.dot(
        w, jnp.broadcast_to(xbar, (depth, LANES)), precision=HIGH, preferred_element_type=jnp.float32
    )
    quad = jnp.dot(w, spread, precision=HIGH, preferred_element_type=jnp.float32) * w
    chan_var = jnp.sum(quad, axis=1, keepdims=True)
    of_row = (lax.broadcasted_iota(jnp.int32, (chans, chans), 0) * 6554) >> 16
    of_col = (lax.broadcasted_iota(jnp.int32, (chans, chans), 1) * 6554) >> 16
    member = (of_row == of_col).astype(jnp.float32)
    mean = jnp.dot(member, chan_mean, precision=HIGH, preferred_element_type=jnp.float32) * 0.1
    off = chan_mean - mean
    var = jnp.dot(member, chan_var + off * off, precision=HIGH, preferred_element_type=jnp.float32) * 0.1
    scale = 0.5 * gain / jnp.sqrt(var + 1e-05)
    base = 0.5 * shift - mean * scale

    phase = phase_ref[0]
    first, last = phase == 0, phase == 3
    scale2 = jnp.concatenate([scale, scale], axis=1)
    base2 = jnp.concatenate([base, base], axis=1)
    pairs = (width + 2) // 2
    for pair in range(pairs):
        start = phase * tile + pair * 2 * LANES
        cells = jnp.concatenate(
            [
                shifted[a, :, pl.ds(pl.multiple_of(start + b * LANES, LANES), 2 * LANES)]
                for a in range(3)
                for b in range(3)
            ],
            axis=0,
        ).astype(jnp.bfloat16)
        feat = jnp.dot(w_bf, cells, preferred_element_type=jnp.float32)
        half = feat * scale2 + base2
        act = half * jnp.tanh(half) + half
        if pair == 0:
            act = jnp.concatenate([jnp.where(first, 0.0, act[:, :LANES]), act[:, LANES:]], axis=1)
        if pair == pairs - 1:
            act = jnp.concatenate([act[:, :LANES], jnp.where(last, 0.0, act[:, LANES:])], axis=1)
        hidden_ref[:, pair * 2 * LANES : (pair + 1) * 2 * LANES] = act.astype(jnp.bfloat16)


def features(phase, window, params, chans):
    width = window.shape[2] // LANES
    return pl.pallas_call(
        features_kernel,
        out_shape=jax.ShapeDtypeStruct((chans, (width + 2) * LANES), jnp.bfloat16),
        in_specs=[pl.BlockSpec(memory_space=pltpu.SMEM)] + [pl.BlockSpec(memory_space=pltpu.VMEM)] * 2,
        out_specs=pl.BlockSpec(memory_space=pltpu.VMEM),
        scratch_shapes=[pltpu.VMEM((3, ROWS, (WIN + 2 * EDGE) * LANES), jnp.float32)],
        compiler_params=pltpu.CompilerParams(vmem_limit_bytes=16 * 2**20),
        name="features",
    )(phase, window, params)


KPAD = 512
COLS = 4
HALF_COLS = 16
BLOCK = 80
VMEM = pl.BlockSpec(memory_space=pltpu.VMEM)
SMEM = pl.BlockSpec(memory_space=pltpu.SMEM)


def split_float(value):
    high = value.astype(jnp.bfloat16).astype(jnp.float32)
    return high, value - high


LOW = pltpu.CompilerParams(vmem_limit_bytes=8 * 2**20)


def prepare_kernel(
    w_conv_ref,
    third_ref,
    latent_ref,
    step_ref,
    one_ref,
    two_ref,
    w_in_ref,
    gain_ref,
    shift_ref,
    shard_ref,
    own_ref,
    params_ref,
    rows,
):
    shard, chans = w_conv_ref.shape[1:]
    half, temb_half = chans // 2, third_ref.shape[1] // 2
    temb = two_ref.shape[1]
    own_ref[...] = latent_ref[...].astype(jnp.bfloat16)
    lat, depth = w_in_ref.shape[1], TAPS * ROWS
    params_ref[...] = jnp.zeros(params_ref.shape, jnp.float32)
    for tap in range(TAPS):
        params_ref[tap * ROWS : tap * ROWS + lat, 0:chans] = w_in_ref[tap].astype(jnp.float32)
    params_ref[depth : depth + 1, 0:chans] = gain_ref[...].reshape(1, chans)
    params_ref[depth + 1 : depth + 2, 0:chans] = shift_ref[...].reshape(1, chans)
    rows[...] = jnp.zeros(rows.shape, jnp.float32)
    wide = rows.shape[1] // 2
    for h in range(2):
        for a in range(3):
            for b in range(3):
                at = h * wide + a * KPAD + b * half
                rows[0:shard, at : at + half] = w_conv_ref[
                    3 * a + b, :, h * half : (h + 1) * half
                ].astype(jnp.float32)
        at = h * wide + 3 * KPAD
        rows[0:shard, at : at + temb_half] = third_ref[:, h * temb_half : (h + 1) * temb_half].astype(
            jnp.float32
        )
    lane = lax.broadcasted_iota(jnp.int32, (8, chans), 1)
    k = jnp.where(lane < half, lane, lane - half).astype(jnp.float32)
    freq = jnp.exp(-jnp.log(jnp.float32(10000.0)) * k / jnp.float32(half))
    angle = step_ref[...].astype(jnp.float32) * freq
    emb = jnp.where(lane < half, jnp.cos(angle), jnp.sin(angle))
    first = lax.dot_general(
        emb,
        one_ref[...].astype(jnp.float32),
        (((1,), (1,)), ((), ())),
        precision=HIGH,
        preferred_element_type=jnp.float32,
    )
    first = (first / (1.0 + jnp.exp(-first))).astype(jnp.bfloat16)
    second = jnp.dot(first, two_ref[...], preferred_element_type=jnp.float32)
    high, low = split_float(second[0:1])
    rows[shard : shard + 1, 0:temb] = high
    rows[shard + 1 : shard + 2, 0:temb] = low
    shard_ref[...] = rows[...].astype(jnp.bfloat16)


def prepare(w_conv, third, latent, step, w_one, w_two, w_in, gain, shift):
    wide = 6 * KPAD + third.shape[1]
    inputs = (w_conv, third, latent, step, w_one, w_two, w_in, gain, shift)
    return pl.pallas_call(
        prepare_kernel,
        out_shape=(
            jax.ShapeDtypeStruct((16, wide), jnp.bfloat16),
            jax.ShapeDtypeStruct(latent.shape, jnp.bfloat16),
            jax.ShapeDtypeStruct((LANES, 3 * LANES), jnp.float32),
        ),
        in_specs=[VMEM] * len(inputs),
        out_specs=(VMEM,) * 3,
        scratch_shapes=[pltpu.VMEM((16, wide), jnp.float32)],
        name="prepare",
    )(*inputs)


def theirs_kernel(place_ref, *rest):
    parts, out_ref = rest[:4], rest[4]
    core, z_lo = place_ref[0], place_ref[1]
    wide = out_ref.shape[2]
    for k in range(4):
        out_ref[(z_lo + k) % 4] = parts[k][:, pl.ds(pl.multiple_of((1 - core) * wide, LANES), wide)]


def for_other_core(place, parts):
    rows, wide = parts[0].shape
    return pl.pallas_call(
        theirs_kernel,
        out_shape=jax.ShapeDtypeStruct((4, rows, wide // 2), parts[0].dtype),
        in_specs=[SMEM] + [VMEM] * 4,
        out_specs=VMEM,
        compiler_params=LOW,
        name="for_other_core",
    )(place, *parts)


def block_kernel(place_ref, got_ref, *rest):
    parts, out_ref, held, rows = rest[:4], rest[4], rest[5], rest[6]
    core, z_lo = place_ref[0], place_ref[1]
    wide = out_ref.shape[1]
    shard = BLOCK // 8
    temb = 2 * (wide - 3 * KPAD)
    total = jnp.zeros((1, temb), jnp.float32)
    for k in range(4):
        part = parts[k][:, pl.ds(pl.multiple_of(core * wide, LANES), wide)]
        held[(z_lo + k) % 4] = part.astype(jnp.float32)
        two = parts[k][:, 0:temb].astype(jnp.float32)
        total = total + two[shard : shard + 1] + two[shard + 1 : shard + 2]
    for k in range(4):
        mine, got = held[k], got_ref[k].astype(jnp.float32)
        at = 2 * shard * k
        rows[at : at + 16, :] = jnp.where(core == 0, mine, got)
        rows[at + shard : at + shard + 16, :] = jnp.where(core == 0, got, mine)
    rows[BLOCK : BLOCK + 8, :] = jnp.zeros((8, wide), jnp.float32)
    high, low = split_float(total)
    rows[BLOCK : BLOCK + 1, :temb] = high
    rows[BLOCK + 1 : BLOCK + 2, :temb] = low
    out_ref[...] = rows[0 : BLOCK + 8, :].astype(jnp.bfloat16)


def make_block(place, got, parts):
    wide = got.shape[2]
    return pl.pallas_call(
        block_kernel,
        out_shape=jax.ShapeDtypeStruct((BLOCK + 8, wide), jnp.bfloat16),
        in_specs=[SMEM] + [VMEM] * 5,
        out_specs=VMEM,
        scratch_shapes=[
            pltpu.VMEM((4, 16, wide), jnp.float32),
            pltpu.VMEM((BLOCK + 16, wide), jnp.float32),
        ],
        compiler_params=LOW,
        name="make_block",
    )(place, got, *parts)


def pick(rows, cols, offset, down):
    source = lax.broadcasted_iota(jnp.int32, (rows, cols), 1 if down else 0)
    target = lax.broadcasted_iota(jnp.int32, (rows, cols), 0 if down else 1)
    return jnp.where(source == target + offset, 1.0, 0.0).astype(jnp.bfloat16)


def strip_kernel(offset_ref, own_ref, beside_ref, out_ref):
    width = own_ref.shape[1]
    chosen = pick(width, 2 * width, offset_ref[...], True)
    for c in range(own_ref.shape[0]):
        both = jnp.concatenate([own_ref[c], beside_ref[c]], axis=0)
        out_ref[c] = jnp.dot(chosen, both, preferred_element_type=jnp.float32).astype(jnp.bfloat16)


def moved_kernel(offset_ref, strip_ref, below_ref, out_ref):
    height = strip_ref.shape[2]
    chosen = pick(2 * height, height, offset_ref[...], False)
    for c in range(strip_ref.shape[0]):
        both = jnp.concatenate([strip_ref[c], below_ref[c]], axis=1)
        out_ref[c] = jnp.dot(both, chosen, preferred_element_type=jnp.float32).astype(jnp.bfloat16)


def shift(kernel, offset, first, second, name):
    return pl.pallas_call(
        kernel,
        out_shape=jax.ShapeDtypeStruct(first.shape, first.dtype),
        in_specs=[VMEM] * 3,
        out_specs=VMEM,
        compiler_params=LOW,
        name=name,
    )(offset.reshape(1, 1), first, second)


def conv_kernel(place_ref, hidden_ref, *rest):
    refs, (out_ref, prod_a, prod_b, wide, staged, sems) = rest[:8], rest[8:]
    prods = (prod_a, prod_b)
    core, xpos = place_ref[0], place_ref[2]
    chans = hidden_ref.shape[0]
    half = chans // 2
    own = pl.multiple_of(core * half, 16)
    other = pl.multiple_of((1 - core) * half, 16)
    n = COLS * LANES
    temb_half = refs[0].shape[1] - 3 * KPAD
    lane = lax.broadcasted_iota(jnp.int32, (BLOCK, n), 1) % LANES

    def block(side, k, first, last):
        return refs[4 * side + k][0:BLOCK, first:last]

    second = jnp.zeros((1, 2 * temb_half), jnp.float32)
    for ref in refs:
        two = ref[BLOCK : BLOCK + 8, 0 : 2 * temb_half].astype(jnp.float32)
        second = second + two[0:1] + two[1:2]
    s_two = second / (1.0 + jnp.exp(-second))
    s_two = s_two.astype(jnp.bfloat16).astype(jnp.float32)
    s_low, s_high = s_two[:, :temb_half], s_two[:, temb_half:]
    s_sides = (jnp.where(core == 0, s_low, s_high), jnp.where(core == 0, s_high, s_low))
    tvecs = []
    for k in range(4):
        terms = [
            block(side, k, 3 * KPAD, 3 * KPAD + temb_half).astype(jnp.float32) * s_sides[side]
            for side in range(2)
        ]
        tvecs.append(jnp.sum(terms[0] + terms[1], axis=1, keepdims=True))

    def multiply(col, prod):
        right = []
        for rows in (own, other):
            for b in range(3):
                at = (col + b) * LANES
                right.append(hidden_ref[pl.ds(rows, half), at : at + n])
            right.append(right[-1][0 : KPAD - 3 * half])
        right = jnp.concatenate(right, axis=0)
        left = jnp.concatenate(
            [
                jnp.concatenate([block(side, k, a * KPAD, (a + 1) * KPAD) for side in range(2)], axis=1)
                for k in range(4)
                for a in range(3)
            ],
            axis=0,
        )
        prod[...] = jnp.dot(left, right, preferred_element_type=jnp.float32)

    def finish(local, prod):
        for k in range(4):
            at = 3 * k * BLOCK
            low = prod[at : at + BLOCK, :]
            mid = prod[at + BLOCK : at + 2 * BLOCK, :]
            high = prod[at + 2 * BLOCK : at + 3 * BLOCK, :]
            done = (
                mid
                + jnp.where(lane == 0, 0.0, pltpu.roll(low, 1, 1))
                + jnp.where(lane == LANES - 1, 0.0, pltpu.roll(high, n - 1, 1))
                + tvecs[k]
            )
            chan = (xpos + (0, 1, 3, 2)[k]) % 4 * BLOCK
            for j in range(COLS):
                first = chan * HALF_COLS + local + j
                wide[pl.ds(first, BLOCK, stride=HALF_COLS), :] = done[:, j * LANES : (j + 1) * LANES]

    width = out_ref.shape[1]
    tiles, per = width // COLS, HALF_COLS // COLS
    copies = []
    for t in range(tiles + 1):
        if t < tiles:
            multiply(t * COLS, prods[t % 2])
        if t > 0:
            finish((t - 1) % per * COLS, prods[(t - 1) % 2])
            if t % per == 0:
                h = t // per - 1
                staged[h] = wide[...].reshape(chans, HALF_COLS, LANES).astype(jnp.bfloat16)
                copy = pltpu.make_async_copy(
                    staged.at[h], out_ref.at[:, pl.ds(h * HALF_COLS, HALF_COLS), :], sems.at[h]
                )
                copy.start()
                copies.append(copy)
    for copy in copies:
        copy.wait()


def conv(place, hidden, pieces):
    chans, padded = hidden.shape
    width = padded // LANES - 2
    halves = width // HALF_COLS
    return pl.pallas_call(
        conv_kernel,
        out_shape=jax.ShapeDtypeStruct((chans, width, LANES), jnp.bfloat16),
        in_specs=[SMEM] + [VMEM] * (1 + len(pieces)),
        out_specs=pl.BlockSpec(memory_space=pl.ANY),
        scratch_shapes=[
            pltpu.VMEM((3 * chans, COLS * LANES), jnp.float32),
            pltpu.VMEM((3 * chans, COLS * LANES), jnp.float32),
            pltpu.VMEM((chans * HALF_COLS, LANES), jnp.float32),
            pltpu.VMEM((halves, chans, HALF_COLS, LANES), jnp.bfloat16),
            pltpu.SemaphoreType.DMA((halves,)),
        ],
        compiler_params=pltpu.CompilerParams(vmem_limit_bytes=20 * 2**20),
        name="convolve",
    )(place, hidden, *pieces)


def pairs_of(move):
    pairs = []
    for row in range(8):
        for col in range(32):
            y, z_hi, x, z_lo, core = row // 2, row % 2, col // 8, col // 2 % 4, col % 2
            z = z_hi * 4 + z_lo
            y, z, x, core = move(y, z, x, core)
            y, z, x = y % 4, z % 8, x % 4
            pairs.append((row * 32 + col, (y * 2 + z // 4) * 32 + x * 8 + z % 4 * 2 + core))
    return pairs


def send(value, move):
    return lax.ppermute(value, ("row", "col"), pairs_of(move))


def fetch_grid(value, rows, cols):
    pairs = [
        ((r + rows) % 8 * 32 + (c + cols) % 32, r * 32 + c) for r in range(8) for c in range(32)
    ]
    return lax.ppermute(value, ("row", "col"), pairs)


def swap_core(value):
    return send(value, lambda y, z, x, core: (y, z, x, 1 - core))


def from_z(value, steps):
    return send(value, lambda y, z, x, core: (y, z - steps, x, core))


def from_x(value, steps):
    return send(value, lambda y, z, x, core: (y, z, x - steps, core))


WINDOW_GROUPS = [[r * 32 + (4 * p + 2 + k) % 32 for k in range(4)] for r in range(8) for p in range(8)]


def body(
    latent,
    row_offset,
    col_offset,
    timestep,
    w_in,
    norm_gain,
    norm_shift,
    w_conv,
    w_time1,
    w_time2,
    w_time3,
):
    chans, lat = w_in.shape[1:]
    width, height = latent.shape[1:]
    col = lax.axis_index("col")
    core, z_lo, x = col % 2, col // 2 % 4, col // 8
    phase = (col + 30) % 4

    shard, own, params = prepare(
        w_conv,
        w_time3.T,
        latent,
        timestep.reshape(1, 1),
        w_time1.T,
        w_time2,
        w_in.transpose(0, 2, 1),
        norm_gain,
        norm_shift,
    )
    beside = fetch_grid(own, 0, 1)
    near = [shard, from_z(shard, 1), from_z(shard, 2), from_z(shard, -1)]
    strip = shift(strip_kernel, col_offset, own, beside, "strip")
    below = fetch_grid(strip, 1, 0)
    place = jnp.stack([core, z_lo, x])
    near, below = lax.optimization_barrier((near, below))
    got = swap_core(for_other_core(place, near))
    block = make_block(place, got, near)
    after, before, across = from_x(block, 1), from_x(block, -1), from_x(block, 2)

    moved = shift(moved_kernel, row_offset, strip, below, "moved")
    window = lax.all_gather(
        moved.reshape(lat, width * height), ("row", "col"), axis_index_groups=WINDOW_GROUPS, axis=0
    )
    hidden = features(phase[None], window, params, chans)
    far = lax.optimization_barrier((after, before, across, hidden))
    after, before, across, hidden = far
    pieces = [block, after, before, across]
    pieces = pieces + [swap_core(v) for v in pieces]
    return conv(place, hidden, pieces)


def solution(mesh):
    return jax.shard_map(
        body,
        mesh=mesh,
        in_specs=(
            P(None, "col", "row"),
            P(),
            P(),
            P(),
            P(),
            P(),
            P(),
            P(None, "col", None),
            P(None, "col"),
            P("col", None),
            P(None, "col"),
        ),
        out_specs=P(None, "col", "row"),
        check_vma=False,
    )
```

time: 84.7 us -> 66.2 us (0.78)
  local copies, waits for them, and re-layouts: 6.73 us -> 2.61 us
  waiting for transfers between devices: 9.85 us -> 5.9 us
  starting transfers between devices: 26.2 us -> 22.4 us
  other arithmetic: 3.05 us -> 0.08 us
  blocking collectives: 12.1 us -> 10.4 us
  matrix products: 1.06 us -> 0 us
    ppermute x12 -> x11, waiting for transfers between devices: 9.84 us -> 3.86 us  [send(): return lax.ppermute(value, ('row', 'col'), pairs_of(move))]
    ppermute x3 -> x2, starting transfers between devices: 12.9 us -> 7.8 us  [fetch_grid(): return lax.ppermute(value, ('row', 'col'), pairs)]
    reshape x7 -> x0, local copies, waits for them, and re-layouts: 2.17 us -> none  [the longest x2 1.06 us: body(): taps = w_conv.reshape(3, 3, shard, 2, chans // 2).transpose(3, 2, 0, 1, 4)]
    ppermute x3 -> x2, waiting for transfers between devices: 0.01 us -> 2.05 us  [fetch_grid(): return lax.ppermute(value, ('row', 'col'), pairs)]
    all_gather x1, blocking collectives: 12.1 us -> 10.4 us  [body(): lax.all_gather(moved.reshape(lat, width * height), ('row', 'col'), axis_i...]
    ppermute x12 -> x11, starting transfers between devices: 13.4 us -> 14.6 us  [send(): return lax.ppermute(value, ('row', 'col'), pairs_of(move))]
    concatenate x3 -> x0, local copies, waits for them, and re-layouts: 1.12 us -> none  [the longest x1 1.1 us: body(): ring = jnp.concatenate([v[:2 * shard] for v in near + near])]
    dot_general x2 -> x0, matrix products: 1.06 us -> none  [the longest x1 0.88 us: body(): jnp.dot(emb, w_time1.astype(jnp.float32), precision=lax.Precision.HIGHEST)]
  transfers between devices with their start and end apart: 15 -> 13, of which waited for: 4 -> 7; matrix products, arithmetic and copies ran while one was open for 5% -> 0% of each run, Pallas kernels for 8% -> 11%
where the time goes in v2:
time: 66.2 us; the launch traced here: 66 us
  Pallas kernels  22.4 us (34%)
  starting transfers between devices  22.4 us (34%)
  blocking collectives  10.4 us (16%)
  waiting for transfers between devices  5.9 us (9%)
  local copies, waits for them, and re-layouts  2.61 us (4%)
  between operations  2.2 us (3%)
    ppermute x11, starting transfers between devices, send(): return lax.ppermute(value, ('row', 'col'), pairs_of(move))  14.6 us
    pallas_call x1, Pallas kernels, conv(): pl.pallas_call(conv_kernel, out_shape=jax.ShapeDtypeStruct((chans, width,...  11.6 us
    all_gather x1, blocking collectives, body(): lax.all_gather(moved.reshape(lat, width * height), ('row', 'col'), axis_i...  10.4 us
    ppermute x2, starting transfers between devices, fetch_grid(): return lax.ppermute(value, ('row', 'col'), pairs)  7.8 us
    pallas_call x1, Pallas kernels, features(): pl.pallas_call(features_kernel, out_shape=jax.ShapeDtypeStruct((chans, (w...  6.86 us
    ppermute x11, waiting for transfers between devices, send(): return lax.ppermute(value, ('row', 'col'), pairs_of(move))  3.86 us
    unnamed x6, local copies, waits for them, and re-layouts  2.58 us
    pallas_call x1, Pallas kernels, prepare(): pl.pallas_call(prepare_kernel, out_shape=(jax.ShapeDtypeStruct((16, wide)...  2.19 us
  transfers between devices with their start and end apart: 13, of which 7 were waited for; matrix products, arithmetic and copies ran while one was open for 0% of the time, Pallas kernels for 11%

profile of v2, /device:TPU:1, one launch (start us, length us, event | category | flops | bytes accessed | tf_op | source)
XLA Modules:
  0.0 66.0 jit_solution(9662500973223262984)
XLA Ops:
  0.7 2.2 %prepare.1 = (bf16[16,4352]{1,0:T(8,128)(2,1)}, bf16[4,32,128]{2,1,0:T(8,128)(2,1)}, f32[128,384]{1,0:T(8,128)}) custom-call(bf16[9,10,320]{2,1,0:T(8,128)(2,1)} %w_conv_ref.1, bf16[10,1280]{1,0:T(8,128)(2,1)} %bitcast.13, f32[4,32,128]{2,1,0:T(8,128)} %latent_ref.1, s32[1,1]{1,0:T(1,128)} %bitcast.12.step_ref, bf16[40,320]{1,0:T(8,128)(2,1)} %bitcast.14, ...), custom_call_target="tpu_custom_call" | custom-call | tf_op jit(solution)/shard_map/prepare/pallas_call | solution.py:206
  2.8 3.2 %collective-permute-start.3 = (bf16[4,32,128]{2,1,0:T(8,128)(2,1)}, bf16[4,32,128]{2,1,0:T(8,128)(2,1)S(1)}, u32[]{:S(2)}, u32[]{:S(2)}) collective-permute-start(bf16[4,32,128]{2,1,0:T(8,128)(2,1)} %get-tuple-element.18.own_ref), channel_id=1, source_target_pairs={{1,0},{2,1},{3,2},{4,3},{5,4},{6,5},{7,6},{8,7},{9,8},{10,9},{11,1... | collective-permute-start | bytes 98312 | tf_op jit(solution)/shard_map/ppermute | solution.py:440
  6.1 0.0 collective-permute-start.2
  6.1 5.0 %collective-permute-start.1 = (bf16[16,4352]{1,0:T(8,128)(2,1)}, bf16[16,4352]{1,0:T(8,128)(2,1)S(1)}, u32[]{:S(2)}, u32[]{:S(2)}) collective-permute-start(bf16[16,4352]{1,0:T(8,128)(2,1)} %get-tuple-element.19.rest_0_), channel_id=1, source_target_pairs={{0,36},{1,37},{2,38},{3,39},{4,0},{5,1},{6,2},{7,3},{8,44},{9,45},... | collective-permute-start | bytes 417800 | tf_op jit(solution)/shard_map/ppermute | solution.py:433
  11.1 0.7 %collective-permute-start = (bf16[16,4352]{1,0:T(8,128)(2,1)}, bf16[16,4352]{1,0:T(8,128)(2,1)S(1)}, u32[]{:S(2)}, u32[]{:S(2)}) collective-permute-start(bf16[16,4352]{1,0:T(8,128)(2,1)} %get-tuple-element.19.rest_0_), channel_id=1, source_target_pairs={{0,38},{1,39},{2,0},{3,1},{4,2},{5,3},{6,4},{7,5},{8,46},{9,47},{1... | collective-permute-start | bytes 417800 | tf_op jit(solution)/shard_map/ppermute | solution.py:433
  12.5 0.0 collective-permute-done.3.beside_ref
  12.5 0.0 copy-start.2
  12.5 0.7 %copy-done.2 = bf16[4,32,128]{2,1,0:T(8,128)(2,1)S(1)} copy-done((bf16[4,32,128]{2,1,0:T(8,128)(2,1)S(1)}, bf16[4,32,128]{2,1,0:T(8,128)(2,1)}, u32[]{:S(2)}) %copy-start.2) | copy-done | bytes 32792
  13.3 0.2 strip.1.strip_ref
  13.5 4.6 %collective-permute-start.4 = (bf16[4,32,128]{2,1,0:T(8,128)(2,1)S(1)}, bf16[4,32,128]{2,1,0:T(8,128)(2,1)S(1)}, u32[]{:S(2)}, u32[]{:S(2)}) collective-permute-start(bf16[4,32,128]{2,1,0:T(8,128)(2,1)S(1)} %strip.1.strip_ref), channel_id=1, source_target_pairs={{32,0},{33,1},{34,2},{35,3},{36,4},{37,5},{38,6},{39,7},{40,8},{41... | collective-permute-start | bytes 98312 | tf_op jit(solution)/shard_map/ppermute | solution.py:440
  18.0 0.1 pad_add_fusion.place_ref
  18.1 2.0 %collective-permute-done.4.below_ref = bf16[4,32,128]{2,1,0:T(8,128)(2,1)S(1)} collective-permute-done((bf16[4,32,128]{2,1,0:T(8,128)(2,1)S(1)}, bf16[4,32,128]{2,1,0:T(8,128)(2,1)S(1)}, u32[]{:S(2)}, u32[]{:S(2)}) %collective-permute-start.4) | collective-permute-done | bytes 32800 | tf_op jit(solution)/shard_map/ppermute | solution.py:440
  20.1 0.0 collective-permute-done.2.rest_3_
  20.1 0.0 collective-permute-done.1.rest_2_
  20.2 0.6 collective-permute-done.rest_1_
  20.8 0.0 copy-start
  20.8 0.9 %copy-done = bf16[16,4352]{1,0:T(8,128)(2,1)S(1)} copy-done((bf16[16,4352]{1,0:T(8,128)(2,1)S(1)}, bf16[16,4352]{1,0:T(8,128)(2,1)}, u32[]{:S(2)}) %copy-start) | copy-done | bytes 139288
  21.7 0.6 for_other_core.1
  22.3 3.4 %collective-permute-start.5 = (bf16[4,16,2176]{2,1,0:T(8,128)(2,1)S(1)}, bf16[4,16,2176]{2,1,0:T(8,128)(2,1)S(1)}, u32[]{:S(2)}, u32[]{:S(2)}) collective-permute-start(bf16[4,16,2176]{2,1,0:T(8,128)(2,1)S(1)} %for_other_core.1), channel_id=1, source_target_pairs={{0,1},{1,0},{2,3},{3,2},{4,5},{5,4},{6,7},{7,6},{8,9},{9,8},{10,11... | collective-permute-start | bytes 835592 | tf_op jit(solution)/shard_map/ppermute | solution.py:433
  25.6 1.2 %collective-permute-done.5.got_ref = bf16[4,16,2176]{2,1,0:T(8,128)(2,1)S(1)} collective-permute-done((bf16[4,16,2176]{2,1,0:T(8,128)(2,1)S(1)}, bf16[4,16,2176]{2,1,0:T(8,128)(2,1)S(1)}, u32[]{:S(2)}, u32[]{:S(2)}) %collective-permute-start.5) | collective-permute-done | bytes 278560 | tf_op jit(solution)/shard_map/ppermute | solution.py:433
  26.8 0.8 %make_block.1.rest_0_ = bf16[88,2176]{1,0:T(8,128)(2,1)S(1)} custom-call(s32[3]{0:T(128)S(1)} %pad_add_fusion.place_ref, bf16[4,16,2176]{2,1,0:T(8,128)(2,1)S(1)} %collective-permute-done.5.got_ref, bf16[16,4352]{1,0:T(8,128)(2,1)S(1)} %copy-done, bf16[16,4352]{1,0:T(8,128)(2,1)S(1)} %collective-permute-done.rest_1_, ...), custom_call_target="tpu_custom_call" | custom-call | tf_op jit(solution)/shard_map/make_block/pallas_call | solution.py:266
  27.6 1.4 %collective-permute-start.8 = (bf16[88,2176]{1,0:T(8,128)(2,1)S(1)}, bf16[88,2176]{1,0:T(8,128)(2,1)S(1)}, u32[]{:S(2)}, u32[]{:S(2)}) collective-permute-start(bf16[88,2176]{1,0:T(8,128)(2,1)S(1)} %make_block.1.rest_0_), channel_id=1, source_target_pairs={{0,16},{1,17},{2,18},{3,19},{4,20},{5,21},{6,22},{7,23},{8,24},{9,... | collective-permute-start | bytes 1148936 | tf_op jit(solution)/shard_map/ppermute | solution.py:433
  29.0 0.3 collective-permute-start.7
  29.3 2.4 %collective-permute-start.6 = (bf16[88,2176]{1,0:T(8,128)(2,1)S(1)}, bf16[88,2176]{1,0:T(8,128)(2,1)S(1)}, u32[]{:S(2)}, u32[]{:S(2)}) collective-permute-start(bf16[88,2176]{1,0:T(8,128)(2,1)S(1)} %make_block.1.rest_0_), channel_id=1, source_target_pairs={{0,24},{1,25},{2,26},{3,27},{4,28},{5,29},{6,30},{7,31},{8,0},{9,1... | collective-permute-start | bytes 1148936 | tf_op jit(solution)/shard_map/ppermute | solution.py:433
  32.3 0.2 moved.1
  32.6 10.4 %all_gather.3.window_ref = bf16[4,4,4096]{2,1,0:T(4,128)(2,1)S(1)} all-gather(bf16[1,4,4096]{2,1,0:T(4,128)(2,1)S(1)} %all_gather_reshape.3), channel_id=1, replica_groups={{2,3,4,5},{6,7,8,9},{10,11,12,13},{14,15,16,17},{18,19,20,21},{22,23,24..., dimensions={0}, use_global_device_ids=true | all-gather | bytes 163840 | tf_op jit(solution)/shard_map/all_gather | solution.py:499
  43.0 0.0 copy-start.1
  43.0 0.9 %copy-done.1 = f32[128,384]{1,0:T(8,128)S(1)} copy-done((f32[128,384]{1,0:T(8,128)S(1)}, f32[128,384]{1,0:T(8,128)}, u32[]{:S(2)}) %copy-start.1) | copy-done | bytes 196632
  43.9 6.9 %features.1.hidden_ref = bf16[320,4352]{1,0:T(8,128)(2,1)S(1)} custom-call(s32[1]{0:T(128)} %bitcast.8.phase_ref, bf16[4,4,4096]{2,1,0:T(4,128)(2,1)S(1)} %all_gather.3.window_ref, f32[128,384]{1,0:T(8,128)S(1)} %copy-done.1), custom_call_target="tpu_custom_call" | custom-call | tf_op jit(solution)/shard_map/features/pallas_call | solution.py:118
  50.8 0.3 collective-permute-start.9
  51.0 0.0 collective-permute-done.8.rest_3_
  51.0 0.0 collective-permute-done.7.rest_2_
  51.1 0.0 collective-permute-done.6.rest_1_
  51.1 0.6 collective-permute-start.10
  51.7 0.2 collective-permute-start.11
  51.8 0.3 collective-permute-start.12
  52.2 0.4 collective-permute-done.9.rest_4_
  52.6 0.5 collective-permute-done.10.rest_5_
  53.1 0.5 collective-permute-done.11.rest_6_
  53.7 0.5 collective-permute-done.12.rest_7_
  54.2 11.6 %convolve.1 = bf16[320,32,128]{2,1,0:T(8,128)(2,1)} custom-call(s32[3]{0:T(128)S(1)} %pad_add_fusion.place_ref, bf16[320,4352]{1,0:T(8,128)(2,1)S(1)} %features.1.hidden_ref, bf16[88,2176]{1,0:T(8,128)(2,1)S(1)} %make_block.1.rest_0_, bf16[88,2176]{1,0:T(8,128)(2,1)S(1)} %collective-permute-done.6.rest_1_, ...), custom_call_target="tpu_custom_call" | custom-call | tf_op jit(solution)/shard_map/convolve/pallas_call | solution.py:403
  (1 shorter events, 0.0 us)
Async XLA Ops:
  2.8 9.7 %collective-permute-start.3 = (bf16[4,32,128]{2,1,0:T(8,128)(2,1)}, bf16[4,32,128]{2,1,0:T(8,128)(2,1)S(1)}, u32[]{:S(2)}, u32[]{:S(2)}) collective-permute-start(bf16[4,32,128]{2,1,0:T(8,128)(2,1)} %get-tuple-element.18.own_ref), channel_id=1, source_target_pairs={{1,0},{2,1},{3,2},{4,3},{5,4},{6,5},{7,6},{8,7},{9,8},{10,9},{11,1... | collective-permute-start | bytes 98312 | tf_op jit(solution)/shard_map/ppermute | solution.py:440
  6.1 14.1 %collective-permute-start.2 = (bf16[16,4352]{1,0:T(8,128)(2,1)}, bf16[16,4352]{1,0:T(8,128)(2,1)S(1)}, u32[]{:S(2)}, u32[]{:S(2)}) collective-permute-start(bf16[16,4352]{1,0:T(8,128)(2,1)} %get-tuple-element.19.rest_0_), channel_id=1, source_target_pairs={{0,2},{1,3},{2,4},{3,5},{4,6},{5,7},{6,32},{7,33},{8,10},{9,11},{1... | collective-permute-start | bytes 417800 | tf_op jit(solution)/shard_map/ppermute | solution.py:433
  6.1 14.1 %collective-permute-start.1 = (bf16[16,4352]{1,0:T(8,128)(2,1)}, bf16[16,4352]{1,0:T(8,128)(2,1)S(1)}, u32[]{:S(2)}, u32[]{:S(2)}) collective-permute-start(bf16[16,4352]{1,0:T(8,128)(2,1)} %get-tuple-element.19.rest_0_), channel_id=1, source_target_pairs={{0,36},{1,37},{2,38},{3,39},{4,0},{5,1},{6,2},{7,3},{8,44},{9,45},... | collective-permute-start | bytes 417800 | tf_op jit(solution)/shard_map/ppermute | solution.py:433
  11.1 9.7 %collective-permute-start = (bf16[16,4352]{1,0:T(8,128)(2,1)}, bf16[16,4352]{1,0:T(8,128)(2,1)S(1)}, u32[]{:S(2)}, u32[]{:S(2)}) collective-permute-start(bf16[16,4352]{1,0:T(8,128)(2,1)} %get-tuple-element.19.rest_0_), channel_id=1, source_target_pairs={{0,38},{1,39},{2,0},{3,1},{4,2},{5,3},{6,4},{7,5},{8,46},{9,47},{1... | collective-permute-start | bytes 417800 | tf_op jit(solution)/shard_map/ppermute | solution.py:433
  12.5 0.8 %copy-start.2 = (bf16[4,32,128]{2,1,0:T(8,128)(2,1)S(1)}, bf16[4,32,128]{2,1,0:T(8,128)(2,1)}, u32[]{:S(2)}) copy-start(bf16[4,32,128]{2,1,0:T(8,128)(2,1)} %get-tuple-element.18.own_ref) | copy-start | bytes 98308
  13.5 6.7 %collective-permute-start.4 = (bf16[4,32,128]{2,1,0:T(8,128)(2,1)S(1)}, bf16[4,32,128]{2,1,0:T(8,128)(2,1)S(1)}, u32[]{:S(2)}, u32[]{:S(2)}) collective-permute-start(bf16[4,32,128]{2,1,0:T(8,128)(2,1)S(1)} %strip.1.strip_ref), channel_id=1, source_target_pairs={{32,0},{33,1},{34,2},{35,3},{36,4},{37,5},{38,6},{39,7},{40,8},{41... | collective-permute-start | bytes 98312 | tf_op jit(solution)/shard_map/ppermute | solution.py:440
  20.8 0.9 %copy-start = (bf16[16,4352]{1,0:T(8,128)(2,1)S(1)}, bf16[16,4352]{1,0:T(8,128)(2,1)}, u32[]{:S(2)}) copy-start(bf16[16,4352]{1,0:T(8,128)(2,1)} %get-tuple-element.19.rest_0_) | copy-start | bytes 417796
  22.3 4.5 %collective-permute-start.5 = (bf16[4,16,2176]{2,1,0:T(8,128)(2,1)S(1)}, bf16[4,16,2176]{2,1,0:T(8,128)(2,1)S(1)}, u32[]{:S(2)}, u32[]{:S(2)}) collective-permute-start(bf16[4,16,2176]{2,1,0:T(8,128)(2,1)S(1)} %for_other_core.1), channel_id=1, source_target_pairs={{0,1},{1,0},{2,3},{3,2},{4,5},{5,4},{6,7},{7,6},{8,9},{9,8},{10,11... | collective-permute-start | bytes 835592 | tf_op jit(solution)/shard_map/ppermute | solution.py:433
  27.6 23.5 %collective-permute-start.8 = (bf16[88,2176]{1,0:T(8,128)(2,1)S(1)}, bf16[88,2176]{1,0:T(8,128)(2,1)S(1)}, u32[]{:S(2)}, u32[]{:S(2)}) collective-permute-start(bf16[88,2176]{1,0:T(8,128)(2,1)S(1)} %make_block.1.rest_0_), channel_id=1, source_target_pairs={{0,16},{1,17},{2,18},{3,19},{4,20},{5,21},{6,22},{7,23},{8,24},{9,... | collective-permute-start | bytes 1148936 | tf_op jit(solution)/shard_map/ppermute | solution.py:433
  29.0 22.1 %collective-permute-start.7 = (bf16[88,2176]{1,0:T(8,128)(2,1)S(1)}, bf16[88,2176]{1,0:T(8,128)(2,1)S(1)}, u32[]{:S(2)}, u32[]{:S(2)}) collective-permute-start(bf16[88,2176]{1,0:T(8,128)(2,1)S(1)} %make_block.1.rest_0_), channel_id=1, source_target_pairs={{0,8},{1,9},{2,10},{3,11},{4,12},{5,13},{6,14},{7,15},{8,16},{9,17... | collective-permute-start | bytes 1148936 | tf_op jit(solution)/shard_map/ppermute | solution.py:433
  29.3 21.8 %collective-permute-start.6 = (bf16[88,2176]{1,0:T(8,128)(2,1)S(1)}, bf16[88,2176]{1,0:T(8,128)(2,1)S(1)}, u32[]{:S(2)}, u32[]{:S(2)}) collective-permute-start(bf16[88,2176]{1,0:T(8,128)(2,1)S(1)} %make_block.1.rest_0_), channel_id=1, source_target_pairs={{0,24},{1,25},{2,26},{3,27},{4,28},{5,29},{6,30},{7,31},{8,0},{9,1... | collective-permute-start | bytes 1148936 | tf_op jit(solution)/shard_map/ppermute | solution.py:433
  43.0 0.9 %copy-start.1 = (f32[128,384]{1,0:T(8,128)S(1)}, f32[128,384]{1,0:T(8,128)}, u32[]{:S(2)}) copy-start(f32[128,384]{1,0:T(8,128)} %get-tuple-element.24.params_ref) | copy-start | bytes 589828
  50.8 1.8 %collective-permute-start.9 = (bf16[88,2176]{1,0:T(8,128)(2,1)S(1)}, bf16[88,2176]{1,0:T(8,128)(2,1)S(1)}, u32[]{:S(2)}, u32[]{:S(2)}) collective-permute-start(bf16[88,2176]{1,0:T(8,128)(2,1)S(1)} %make_block.1.rest_0_), channel_id=1, source_target_pairs={{0,1},{1,0},{2,3},{3,2},{4,5},{5,4},{6,7},{7,6},{8,9},{9,8},{10,11... | collective-permute-start | bytes 1148936 | tf_op jit(solution)/shard_map/ppermute | solution.py:433
  51.1 2.1 %collective-permute-start.10 = (bf16[88,2176]{1,0:T(8,128)(2,1)S(1)}, bf16[88,2176]{1,0:T(8,128)(2,1)S(1)}, u32[]{:S(2)}, u32[]{:S(2)}) collective-permute-start(bf16[88,2176]{1,0:T(8,128)(2,1)S(1)} %collective-permute-done.6.rest_1_), channel_id=1, source_target_pairs={{0,1},{1,0},{2,3},{3,2},{4,5},{5,4},{6,7},{7,6},{8,9},{9,8},{10,11... | collective-permute-start | bytes 1148936 | tf_op jit(solution)/shard_map/ppermute | solution.py:433
  51.7 2.0 %collective-permute-start.11 = (bf16[88,2176]{1,0:T(8,128)(2,1)S(1)}, bf16[88,2176]{1,0:T(8,128)(2,1)S(1)}, u32[]{:S(2)}, u32[]{:S(2)}) collective-permute-start(bf16[88,2176]{1,0:T(8,128)(2,1)S(1)} %collective-permute-done.7.rest_2_), channel_id=1, source_target_pairs={{0,1},{1,0},{2,3},{3,2},{4,5},{5,4},{6,7},{7,6},{8,9},{9,8},{10,11... | collective-permute-start | bytes 1148936 | tf_op jit(solution)/shard_map/ppermute | solution.py:433
  51.8 2.4 %collective-permute-start.12 = (bf16[88,2176]{1,0:T(8,128)(2,1)S(1)}, bf16[88,2176]{1,0:T(8,128)(2,1)S(1)}, u32[]{:S(2)}, u32[]{:S(2)}) collective-permute-start(bf16[88,2176]{1,0:T(8,128)(2,1)S(1)} %collective-permute-done.8.rest_3_), channel_id=1, source_target_pairs={{0,1},{1,0},{2,3},{3,2},{4,5},{5,4},{6,7},{7,6},{8,9},{9,8},{10,11... | collective-permute-start | bytes 1148936 | tf_op jit(solution)/shard_map/ppermute | solution.py:433

commit v3 on v2

v3 whole, which is shorter than its diff:
```python
import jax
import jax.numpy as jnp
from jax import lax
from jax.experimental import pallas as pl
from jax.experimental.pallas import tpu as pltpu
from jax.sharding import PartitionSpec as P

WIN = 128
LANES = 128
EDGE = 2
HIGH = lax.Precision.HIGHEST
ROWS = 8
DEPTH = 6 * ROWS


def features_kernel(window_ref, params_ref, hidden_ref, shifted):
    chans = hidden_ref.shape[0]
    tile = window_ref.shape[2]
    width = tile // LANES
    lat = window_ref.shape[1]
    span = WIN * LANES
    total = span + 2 * EDGE * LANES
    lane = lax.broadcasted_iota(jnp.int32, (ROWS, tile), 1) % LANES
    zeros_edge = jnp.zeros((ROWS, EDGE * LANES), jnp.float32)
    for a in range(3):
        shifted[a, :, 0 : EDGE * LANES] = zeros_edge
        shifted[a, :, total - EDGE * LANES : total] = zeros_edge
        shifted[a, :, total - (EDGE + 1) * LANES : total - EDGE * LANES] = zeros_edge[:, :LANES]
    for part in range(window_ref.shape[0]):
        cells = window_ref[part].astype(jnp.float32)
        cells = jnp.concatenate([cells, cells], axis=0)
        at = EDGE * LANES + part * tile
        views = (
            jnp.where(lane == 0, 0.0, pltpu.roll(cells, 1, 1)),
            cells,
            jnp.where(lane == LANES - 1, 0.0, pltpu.roll(cells, tile - 1, 1)),
        )
        for a, view in enumerate(views):
            shifted[a, 0:lat, at : at + tile] = view[0:lat]
            shifted[a, lat : 2 * lat, at - LANES : at + tile - LANES] = view[lat : 2 * lat]

    def patches(start, size):
        return jnp.concatenate(
            [shifted[a, :, pl.ds(start + 2 * b * LANES, size)] for a in range(3) for b in range(2)],
            axis=0,
        )

    depth = DEPTH
    columns = params_ref[...].T
    w = columns[0:chans, 0:depth]
    w_bf = w.astype(jnp.bfloat16)
    gain = jnp.broadcast_to(columns[0:chans, depth : depth + 1], (chans, LANES))
    shift = jnp.broadcast_to(columns[0:chans, depth + 1 : depth + 2], (chans, LANES))
    count = float(span)
    first_cell = (EDGE - 1) * LANES
    xbar = jnp.sum(patches(first_cell, span), axis=1, keepdims=True) * (1.0 / count)
    same = jnp.zeros((depth, depth), jnp.float32)
    cross = same
    chunk = 2048
    dims = (((1,), (1,)), ((), ()))
    for step in range(span // chunk):
        centred = patches(first_cell + step * chunk, chunk) - xbar
        high = centred.astype(jnp.bfloat16)
        low = (centred - high.astype(jnp.float32)).astype(jnp.bfloat16)
        same = same + lax.dot_general(high, high, dims, preferred_element_type=jnp.float32)
        cross = cross + lax.dot_general(high, low, dims, preferred_element_type=jnp.float32)
    spread = (same + 2.0 * cross) * (1.0 / count)
    chan_mean = jnp.dot(
        w, jnp.broadcast_to(xbar, (depth, LANES)), precision=HIGH, preferred_element_type=jnp.float32
    )
    quad = jnp.dot(w, spread, precision=HIGH, preferred_element_type=jnp.float32) * w
    chan_var = jnp.sum(quad, axis=1, keepdims=True)
    of_row = (lax.broadcasted_iota(jnp.int32, (chans, chans), 0) * 6554) >> 16
    of_col = (lax.broadcasted_iota(jnp.int32, (chans, chans), 1) * 6554) >> 16
    member = (of_row == of_col).astype(jnp.float32)
    mean = jnp.dot(member, chan_mean, precision=HIGH, preferred_element_type=jnp.float32) * 0.1
    off = chan_mean - mean
    var = jnp.dot(member, chan_var + off * off, precision=HIGH, preferred_element_type=jnp.float32) * 0.1
    scale = 0.5 * gain / jnp.sqrt(var + 1e-05)
    base = 0.5 * shift - mean * scale

    phase = lax.rem(lax.axis_index("col") + 30, 4)
    first, last = phase == 0, phase == 3
    scale2 = jnp.concatenate([scale, scale], axis=1)
    base2 = jnp.concatenate([base, base], axis=1)
    pairs = (width + 2) // 2
    for pair in range(pairs):
        start = phase * tile + pair * 2 * LANES
        cells = jnp.concatenate(
            [
                shifted[a, :, pl.ds(pl.multiple_of(start + 2 * b * LANES, LANES), 2 * LANES)]
                for a in range(3)
                for b in range(2)
            ],
            axis=0,
        ).astype(jnp.bfloat16)
        feat = jnp.dot(w_bf, cells, preferred_element_type=jnp.float32)
        half = feat * scale2 + base2
        act = half * jnp.tanh(half) + half
        if pair == 0:
            act = jnp.concatenate([jnp.where(first, 0.0, act[:, :LANES]), act[:, LANES:]], axis=1)
        if pair == pairs - 1:
            act = jnp.concatenate([act[:, :LANES], jnp.where(last, 0.0, act[:, LANES:])], axis=1)
        hidden_ref[:, pair * 2 * LANES : (pair + 1) * 2 * LANES] = act.astype(jnp.bfloat16)


def features(window, params, chans):
    width = window.shape[2] // LANES
    return pl.pallas_call(
        features_kernel,
        out_shape=jax.ShapeDtypeStruct((chans, (width + 2) * LANES), jnp.bfloat16),
        in_specs=[pl.BlockSpec(memory_space=pltpu.VMEM)] * 2,
        out_specs=pl.BlockSpec(memory_space=pltpu.VMEM),
        scratch_shapes=[pltpu.VMEM((3, ROWS, (WIN + 2 * EDGE) * LANES), jnp.float32)],
        compiler_params=pltpu.CompilerParams(vmem_limit_bytes=16 * 2**20),
        name="features",
    )(in_vmem(window), in_vmem(params))


KPAD = 512
COLS = 4
HALF_COLS = 16
BLOCK = 80
VMEM = pl.BlockSpec(memory_space=pltpu.VMEM)
SMEM = pl.BlockSpec(memory_space=pltpu.SMEM)


def position():
    col = lax.axis_index("col")
    return lax.rem(col, 2), lax.rem(lax.div(col, 2), 4), lax.div(col, 8)


def in_vmem(value):
    return pltpu.with_memory_space_constraint(value, pltpu.VMEM)


def split_float(value):
    high = value.astype(jnp.bfloat16).astype(jnp.float32)
    return high, value - high


LOW = pltpu.CompilerParams(vmem_limit_bytes=8 * 2**20)


def prepare_kernel(*rest):
    w_conv_ref, third_ref, latent_ref, one_ref, two_ref, w_in_ref = rest[15:21]
    gain_ref, shift_ref, steps_ref = rest[21:24]
    rows, sems = rest[24:]
    copies = [pltpu.make_async_copy(rest[i], rest[15 + i], sems.at[i]) for i in range(9)]
    for copy in copies:
        copy.start()
    mine_ref, theirs_ref, own_ref, part_ref, params_ref, offsets_ref = rest[9:15]
    core, _, _ = position()
    shard, chans = w_conv_ref.shape[1:]
    half, temb_half = chans // 2, third_ref.shape[1] // 2
    rows[...] = jnp.zeros(rows.shape, jnp.float32)
    params_ref[...] = jnp.zeros(params_ref.shape, jnp.float32)
    lane = lax.broadcasted_iota(jnp.int32, (8, chans), 1)
    k = jnp.where(lane < half, lane, lane - half).astype(jnp.float32)
    freq = jnp.exp(-jnp.log(jnp.float32(10000.0)) * k / jnp.float32(half))
    for copy in copies:
        copy.wait()
    offsets_ref[...] = steps_ref[...]
    own_ref[...] = latent_ref[...].astype(jnp.bfloat16)
    for h in range(2):
        for a in range(3):
            for b in range(3):
                at = a * KPAD + b * half
                rows[h, 0:shard, at : at + half] = w_conv_ref[
                    3 * a + b, :, h * half : (h + 1) * half
                ].astype(jnp.float32)
        rows[h, 0:shard, 3 * KPAD :] = third_ref[:, h * temb_half : (h + 1) * temb_half].astype(
            jnp.float32
        )
    mine_ref[...] = rows[core].astype(jnp.bfloat16)
    theirs_ref[...] = rows[1 - core].astype(jnp.bfloat16)
    lat, depth = w_in_ref.shape[1], DEPTH
    for tap in range(w_in_ref.shape[0]):
        at = tap // 3 * 2 * ROWS + tap % 3 * lat
        params_ref[at : at + lat, 0:chans] = w_in_ref[tap].astype(jnp.float32)
    params_ref[depth : depth + 1, 0:chans] = gain_ref[...].reshape(1, chans)
    params_ref[depth + 1 : depth + 2, 0:chans] = shift_ref[...].reshape(1, chans)
    angle = steps_ref[2:3, 0:1].astype(jnp.float32) * freq
    emb = jnp.where(lane < half, jnp.cos(angle), jnp.sin(angle))
    first = lax.dot_general(
        emb,
        one_ref[...].astype(jnp.float32),
        (((1,), (1,)), ((), ())),
        precision=HIGH,
        preferred_element_type=jnp.float32,
    )
    first = (first / (1.0 + jnp.exp(-first))).astype(jnp.bfloat16)
    second = jnp.dot(first, two_ref[...], preferred_element_type=jnp.float32)
    high, low = split_float(second)
    row = lax.broadcasted_iota(jnp.int32, second.shape, 0)
    part_ref[...] = jnp.where(row == 0, high, jnp.where(row == 1, low, 0.0))


def prepare(w_conv, third, latent, w_one, w_two, w_in, gain, shift, steps):
    wide = 3 * KPAD + third.shape[1] // 2
    inputs = (w_conv, third, latent, w_one, w_two, w_in, gain, shift, steps)
    inputs = [pltpu.with_memory_space_constraint(v, pltpu.HBM) for v in inputs]
    return pl.pallas_call(
        prepare_kernel,
        out_shape=(
            jax.ShapeDtypeStruct((16, wide), jnp.bfloat16),
            jax.ShapeDtypeStruct((16, wide), jnp.bfloat16),
            jax.ShapeDtypeStruct(latent.shape, jnp.bfloat16),
            jax.ShapeDtypeStruct((8, w_two.shape[1]), jnp.float32),
            jax.ShapeDtypeStruct((LANES, 3 * LANES), jnp.float32),
            jax.ShapeDtypeStruct(steps.shape, steps.dtype),
        ),
        in_specs=[pl.BlockSpec(memory_space=pltpu.HBM)] * len(inputs),
        out_specs=(VMEM,) * 6,
        scratch_shapes=[pltpu.VMEM(v.shape, v.dtype) for v in inputs]
        + [pltpu.VMEM((2, 16, wide), jnp.float32), pltpu.SemaphoreType.DMA((len(inputs),))],
        compiler_params=LOW,
        name="prepare",
    )(*inputs)


def pair_kernel(mine_ref, got_ref, time_ref, out_ref, rows):
    core, _, _ = position()
    shard = 10
    temb = time_ref.shape[1]
    mine = mine_ref[...].astype(jnp.float32)
    got = got_ref[...].astype(jnp.float32)
    rows[0:16, :] = jnp.where(core == 0, mine, got)
    rows[shard : shard + 16, :] = jnp.where(core == 0, got, mine)
    rows[2 * shard : 2 * shard + 8, 0:temb] = time_ref[...]
    out_ref[...] = rows[0:24, :].astype(jnp.bfloat16)


def pair_up(mine, got, part):
    wide = mine.shape[1]
    return pl.pallas_call(
        pair_kernel,
        out_shape=jax.ShapeDtypeStruct((24, wide), jnp.bfloat16),
        in_specs=[VMEM] * 3,
        out_specs=VMEM,
        scratch_shapes=[pltpu.VMEM((32, wide), jnp.float32)],
        compiler_params=LOW,
        name="pair_up",
    )(in_vmem(mine), in_vmem(got), in_vmem(part))


def block_kernel(*rest):
    parts, out_ref, held, rows = rest[:4], rest[4], rest[5], rest[6]
    _, z_lo, _ = position()
    temb = 1280
    total = jnp.zeros((1, temb), jnp.float32)
    for k in range(4):
        part = parts[k][...].astype(jnp.float32)
        total = total + part[20:21, :temb] + part[21:22, :temb]
        held[(z_lo + k) % 4] = part
    for k in range(4):
        rows[20 * k : 20 * k + 24, :] = held[k]
    rows[80:88, :] = jnp.zeros((8, rows.shape[1]), jnp.float32)
    high, low = split_float(total)
    rows[80:81, :temb] = high
    rows[81:82, :temb] = low
    out_ref[...] = rows[...].astype(jnp.bfloat16)


def make_block(parts):
    wide = parts[0].shape[1]
    return pl.pallas_call(
        block_kernel,
        out_shape=jax.ShapeDtypeStruct((88, wide), jnp.bfloat16),
        in_specs=[VMEM] * 4,
        out_specs=VMEM,
        scratch_shapes=[pltpu.VMEM((4, 24, wide), jnp.float32), pltpu.VMEM((88, wide), jnp.float32)],
        compiler_params=LOW,
        name="make_block",
    )(*[in_vmem(v) for v in parts])


def pick(rows, cols, offset, down):
    source = lax.broadcasted_iota(jnp.int32, (rows, cols), 1 if down else 0)
    target = lax.broadcasted_iota(jnp.int32, (rows, cols), 0 if down else 1)
    return jnp.where(source == target + offset, 1.0, 0.0).astype(jnp.bfloat16)


def strip_kernel(offset_ref, own_ref, beside_ref, out_ref):
    width = own_ref.shape[1]
    chosen = pick(width, 2 * width, offset_ref[1:2, 0:1], True)
    for c in range(own_ref.shape[0]):
        both = jnp.concatenate([own_ref[c], beside_ref[c]], axis=0)
        out_ref[c] = jnp.dot(chosen, both, preferred_element_type=jnp.float32).astype(jnp.bfloat16)


def moved_kernel(offset_ref, strip_ref, below_ref, out_ref, stacked, flat):
    lat, width, height = strip_ref.shape
    chosen = pick(2 * height, height, offset_ref[0:1, 0:1], False)
    for c in range(lat):
        both = jnp.concatenate([strip_ref[c], below_ref[c]], axis=1)
        stacked[c * width : (c + 1) * width, :] = jnp.dot(
            both, chosen, preferred_element_type=jnp.float32
        )
    for j in range(width):
        flat[0:lat, j * height : (j + 1) * height] = stacked[pl.ds(j, lat, stride=width), :]
    out_ref[0] = flat[0:lat, :].astype(jnp.bfloat16)


def shift_columns(offset, own, beside):
    return pl.pallas_call(
        strip_kernel,
        out_shape=jax.ShapeDtypeStruct(own.shape, own.dtype),
        in_specs=[VMEM] * 3,
        out_specs=VMEM,
        compiler_params=LOW,
        name="strip",
    )(in_vmem(offset), in_vmem(own), in_vmem(beside))


def shift_rows(offset, strip, below):
    lat, width, height = strip.shape
    return pl.pallas_call(
        moved_kernel,
        out_shape=jax.ShapeDtypeStruct((1, lat, width * height), strip.dtype),
        in_specs=[VMEM] * 3,
        out_specs=VMEM,
        scratch_shapes=[
            pltpu.VMEM((lat * width, height), jnp.float32),
            pltpu.VMEM((ROWS, width * height), jnp.float32),
        ],
        compiler_params=LOW,
        name="moved",
    )(in_vmem(offset), in_vmem(strip), in_vmem(below))


def conv_kernel(hidden_ref, *rest):
    refs, (out_ref, prod_a, prod_b, wide, staged, sems) = rest[:8], rest[8:]
    prods = (prod_a, prod_b)
    core, _, xpos = position()
    chans = hidden_ref.shape[0]
    half = chans // 2
    own = pl.multiple_of(core * half, 16)
    other = pl.multiple_of((1 - core) * half, 16)
    n = COLS * LANES
    temb_half = refs[0].shape[1] - 3 * KPAD
    lane = lax.broadcasted_iota(jnp.int32, (BLOCK, n), 1) % LANES

    def block(side, k, first, last):
        return refs[4 * side + k][0:BLOCK, first:last]

    second = jnp.zeros((1, 2 * temb_half), jnp.float32)
    for ref in refs:
        two = ref[BLOCK : BLOCK + 8, 0 : 2 * temb_half].astype(jnp.float32)
        second = second + two[0:1] + two[1:2]
    s_two = second / (1.0 + jnp.exp(-second))
    s_two = s_two.astype(jnp.bfloat16).astype(jnp.float32)
    s_low, s_high = s_two[:, :temb_half], s_two[:, temb_half:]
    s_sides = (jnp.where(core == 0, s_low, s_high), jnp.where(core == 0, s_high, s_low))
    tvecs = []
    for k in range(4):
        terms = [
            block(side, k, 3 * KPAD, 3 * KPAD + temb_half).astype(jnp.float32) * s_sides[side]
            for side in range(2)
        ]
        tvecs.append(jnp.sum(terms[0] + terms[1], axis=1, keepdims=True))

    def multiply(col, prod):
        right = []
        for rows in (own, other):
            for b in range(3):
                at = (col + b) * LANES
                right.append(hidden_ref[pl.ds(rows, half), at : at + n])
            right.append(right[-1][0 : KPAD - 3 * half])
        right = jnp.concatenate(right, axis=0)
        left = jnp.concatenate(
            [
                jnp.concatenate([block(side, k, a * KPAD, (a + 1) * KPAD) for side in range(2)], axis=1)
                for k in range(4)
                for a in range(3)
            ],
            axis=0,
        )
        prod[...] = jnp.dot(left, right, preferred_element_type=jnp.float32)

    def finish(local, prod):
        for k in range(4):
            at = 3 * k * BLOCK
            low = prod[at : at + BLOCK, :]
            mid = prod[at + BLOCK : at + 2 * BLOCK, :]
            high = prod[at + 2 * BLOCK : at + 3 * BLOCK, :]
            done = (
                mid
                + jnp.where(lane == 0, 0.0, pltpu.roll(low, 1, 1))
                + jnp.where(lane == LANES - 1, 0.0, pltpu.roll(high, n - 1, 1))
                + tvecs[k]
            )
            chan = (xpos + (0, 1, 3, 2)[k]) % 4 * BLOCK
            for j in range(COLS):
                first = chan * HALF_COLS + local + j
                wide[pl.ds(first, BLOCK, stride=HALF_COLS), :] = done[:, j * LANES : (j + 1) * LANES]

    width = out_ref.shape[1]
    tiles, per = width // COLS, HALF_COLS // COLS
    copies = []
    for t in range(tiles + 1):
        if t < tiles:
            multiply(t * COLS, prods[t % 2])
        if t > 0:
            finish((t - 1) % per * COLS, prods[(t - 1) % 2])
            if t % per == 0:
                h = t // per - 1
                parts = 1 if t < tiles else 4
                size = chans // parts
                for part in range(parts):
                    at = part * size
                    cells = wide[at * HALF_COLS : (at + size) * HALF_COLS, :]
                    staged[h, at : at + size] = cells.reshape(size, HALF_COLS, LANES).astype(jnp.bfloat16)
                    copy = pltpu.make_async_copy(
                        staged.at[h, pl.ds(at, size)],
                        out_ref.at[pl.ds(at, size), pl.ds(h * HALF_COLS, HALF_COLS), :],
                        sems.at[len(copies)],
                    )
                    copy.start()
                    copies.append(copy)
    for copy in copies:
        copy.wait()


def conv(hidden, pieces):
    chans, padded = hidden.shape
    width = padded // LANES - 2
    halves = width // HALF_COLS
    return pl.pallas_call(
        conv_kernel,
        out_shape=jax.ShapeDtypeStruct((chans, width, LANES), jnp.bfloat16),
        in_specs=[VMEM] * (1 + len(pieces)),
        out_specs=pl.BlockSpec(memory_space=pl.ANY),
        scratch_shapes=[
            pltpu.VMEM((3 * chans, COLS * LANES), jnp.float32),
            pltpu.VMEM((3 * chans, COLS * LANES), jnp.float32),
            pltpu.VMEM((chans * HALF_COLS, LANES), jnp.float32),
            pltpu.VMEM((halves, chans, HALF_COLS, LANES), jnp.bfloat16),
            pltpu.SemaphoreType.DMA((halves + 3,)),
        ],
        compiler_params=pltpu.CompilerParams(vmem_limit_bytes=20 * 2**20),
        name="convolve",
    )(in_vmem(hidden), *[in_vmem(v) for v in pieces])


def pairs_of(move):
    pairs = []
    for row in range(8):
        for col in range(32):
            y, z_hi, x, z_lo, core = row // 2, row % 2, col // 8, col // 2 % 4, col % 2
            z = z_hi * 4 + z_lo
            y, z, x, core = move(y, z, x, core)
            y, z, x = y % 4, z % 8, x % 4
            pairs.append((row * 32 + col, (y * 2 + z // 4) * 32 + x * 8 + z % 4 * 2 + core))
    return pairs


def send(value, move):
    return lax.ppermute(value, ("row", "col"), pairs_of(move))


def fetch_grid(value, rows, cols):
    pairs = [
        ((r + rows) % 8 * 32 + (c + cols) % 32, r * 32 + c) for r in range(8) for c in range(32)
    ]
    return lax.ppermute(value, ("row", "col"), pairs)


def swap_core(value):
    return send(value, lambda y, z, x, core: (y, z, x, 1 - core))


def from_z(value, steps):
    return send(value, lambda y, z, x, core: (y, z - steps, x, core))


def from_x(value, steps):
    return send(value, lambda y, z, x, core: (y, z, x - steps, core))


WINDOW_GROUPS = [[r * 32 + (4 * p + 2 + k) % 32 for k in range(4)] for r in range(8) for p in range(8)]


def body(
    latent,
    row_offset,
    col_offset,
    timestep,
    w_in,
    norm_gain,
    norm_shift,
    w_conv,
    w_time1,
    w_time2,
    w_time3,
):
    chans = w_in.shape[1]
    row = lax.broadcasted_iota(jnp.int32, (8, LANES), 0)
    steps = jnp.where(row == 0, row_offset[:, None], jnp.where(row == 1, col_offset[:, None], timestep[:, None]))
    mine, theirs, own, part, params, offsets = prepare(
        w_conv,
        w_time3.T,
        latent,
        w_time1.T,
        w_time2,
        w_in.transpose(0, 2, 1),
        norm_gain,
        norm_shift,
        steps,
    )
    beside = fetch_grid(own, 0, 1)
    got = swap_core(theirs)
    got, beside = lax.optimization_barrier((got, beside))
    zrow = pair_up(mine, got, part)
    near = [zrow, from_z(zrow, 1), from_z(zrow, 2), from_z(zrow, -1)]
    strip = shift_columns(offsets, own, beside)
    below = fetch_grid(strip, 1, 0)
    near, below = lax.optimization_barrier((near, below))
    block = make_block(near)
    after, before, across = from_x(block, 1), from_x(block, -1), from_x(block, 2)

    moved = shift_rows(offsets, strip, below)
    window = lax.all_gather(
        moved, ("row", "col"), axis_index_groups=WINDOW_GROUPS, axis=0, tiled=True
    )
    hidden = features(window, params, chans)
    far = lax.optimization_barrier((after, before, across, hidden))
    after, before, across, hidden = far
    pieces = [block, after, before, across]
    pieces = pieces + [swap_core(v) for v in pieces]
    return conv(hidden, pieces)


def solution(mesh):
    return jax.shard_map(
        body,
        mesh=mesh,
        in_specs=(
            P(None, "col", "row"),
            P(),
            P(),
            P(),
            P(),
            P(),
            P(),
            P(None, "col", None),
            P(None, "col"),
            P("col", None),
            P(None, "col"),
        ),
        out_specs=P(None, "col", "row"),
        check_vma=False,
    )
```

time: 66.2 us -> 62.9 us (0.950)
  the two profiles are of different devices: /device:TPU:1 before, /device:TPU:49 now
where the time goes in v3:
time: 62.9 us; the launch traced here: 62.7 us
  starting transfers between devices  21.7 us (34%)
  Pallas kernels  17.3 us (28%)
  waiting for transfers between devices  15.7 us (25%)
  blocking collectives  5.26 us (8%)
  between operations  2.17 us (3%)
  other arithmetic  0.68 us (1%)
    ppermute x11, starting transfers between devices, send(): return lax.ppermute(value, ('row', 'col'), pairs_of(move))  20.3 us
    pallas_call x1, Pallas kernels, conv(): pl.pallas_call(conv_kernel, out_shape=jax.ShapeDtypeStruct((chans, width,...  11.1 us
    ppermute x2, waiting for transfers between devices, fetch_grid(): return lax.ppermute(value, ('row', 'col'), pairs)  9.09 us
    ppermute x11, waiting for transfers between devices, send(): return lax.ppermute(value, ('row', 'col'), pairs_of(move))  6.56 us
    all_gather x1, blocking collectives, body(): lax.all_gather(moved, ('row', 'col'), axis_index_groups=WINDOW_GROUPS, ax...  5.26 us
    pallas_call x1, Pallas kernels, features(): pl.pallas_call(features_kernel, out_shape=jax.ShapeDtypeStruct((chans, (w...  4.04 us
    pallas_call x1, Pallas kernels, prepare(): pl.pallas_call(prepare_kernel, out_shape=(jax.ShapeDtypeStruct((16, wide)...  1.55 us
    ppermute x2, starting transfers between devices, fetch_grid(): return lax.ppermute(value, ('row', 'col'), pairs)  1.36 us
  transfers between devices with their start and end apart: 13, of which 7 were waited for; matrix products, arithmetic and copies ran while one was open for 0% of the time, Pallas kernels for 7%

profile of v3, /device:TPU:49, one launch (start us, length us, event | category | flops | bytes accessed | tf_op | source)
XLA Modules:
  0.0 62.7 jit_solution(2545620793701737892)
XLA Ops:
  2.0 0.7 %broadcast_select_fusion.rest_8_ = s32[8,128]{1,0:T(8,128)} fusion(s32[8]{0:T(128)S(1)} %compare_select_fusion, s32[]{:T(128)} %bitcast.6, pred[8]{0:T(512)(128)(4,1)S(1)} %iota_compare_fusion), kind=kLoop, calls=%fused_computation | loop fusion | flops 1024 | bytes 4140 | tf_op jit(solution)/shard_map/jit(_where)/select_n | solution.py:499
  2.6 1.5 %prepare.1 = (bf16[16,2176]{1,0:T(8,128)(2,1)S(1)}, bf16[16,2176]{1,0:T(8,128)(2,1)S(1)}, bf16[4,32,128]{2,1,0:T(8,128)(2,1)S(1)}, f32[8,1280]{1,0:T(8,128)S(1)}...) custom-call(bf16[9,10,320]{2,1,0:T(8,128)(2,1)} %rest_0_.1, bf16[10,1280]{1,0:T(8,128)(2,1)} %bitcast.9, ...), custom_call_target="tpu_custom_call" | custom-call | tf_op jit(solution)/shard_map/prepare/pallas_call | solution.py:203
  4.2 0.8 %collective-permute-start = (bf16[16,2176]{1,0:T(8,128)(2,1)S(1)}, bf16[16,2176]{1,0:T(8,128)(2,1)S(1)}, u32[]{:S(2)}, u32[]{:S(2)}) collective-permute-start(bf16[16,2176]{1,0:T(8,128)(2,1)S(1)} %get-tuple-element.23), channel_id=1, source_target_pairs={{0,1},{1,0},{2,3},{3,2},{4,5},{5,4},{6,7},{7,6},{8,9},{9,8},{10,11... | collective-permute-start | bytes 208904 | tf_op jit(solution)/shard_map/ppermute | solution.py:459
  5.0 0.1 collective-permute-start.1
  5.0 3.2 %collective-permute-done.1.beside_ref = bf16[4,32,128]{2,1,0:T(8,128)(2,1)S(1)} collective-permute-done((bf16[4,32,128]{2,1,0:T(8,128)(2,1)S(1)}, bf16[4,32,128]{2,1,0:T(8,128)(2,1)S(1)}, u32[]{:S(2)}, u32[]{:S(2)}) %collective-permute-start.1) | collective-permute-done | bytes 32800 | tf_op jit(solution)/shard_map/ppermute | solution.py:466
  8.3 0.0 collective-permute-done.got_ref
  8.3 0.1 pair_up.1.rest_0_
  8.4 1.7 %collective-permute-start.4 = (bf16[24,2176]{1,0:T(8,128)(2,1)S(1)}, bf16[24,2176]{1,0:T(8,128)(2,1)S(1)}, u32[]{:S(2)}, u32[]{:S(2)}) collective-permute-start(bf16[24,2176]{1,0:T(8,128)(2,1)S(1)} %pair_up.1.rest_0_), channel_id=1, source_target_pairs={{0,2},{1,3},{2,4},{3,5},{4,6},{5,7},{6,32},{7,33},{8,10},{9,11},{1... | collective-permute-start | bytes 313352 | tf_op jit(solution)/shard_map/ppermute | solution.py:459
  10.1 6.3 %collective-permute-start.3 = (bf16[24,2176]{1,0:T(8,128)(2,1)S(1)}, bf16[24,2176]{1,0:T(8,128)(2,1)S(1)}, u32[]{:S(2)}, u32[]{:S(2)}) collective-permute-start(bf16[24,2176]{1,0:T(8,128)(2,1)S(1)} %pair_up.1.rest_0_), channel_id=1, source_target_pairs={{0,36},{1,37},{2,38},{3,39},{4,0},{5,1},{6,2},{7,3},{8,44},{9,45},... | collective-permute-start | bytes 313352 | tf_op jit(solution)/shard_map/ppermute | solution.py:459
  16.3 1.4 %collective-permute-start.2 = (bf16[24,2176]{1,0:T(8,128)(2,1)S(1)}, bf16[24,2176]{1,0:T(8,128)(2,1)S(1)}, u32[]{:S(2)}, u32[]{:S(2)}) collective-permute-start(bf16[24,2176]{1,0:T(8,128)(2,1)S(1)} %pair_up.1.rest_0_), channel_id=1, source_target_pairs={{0,38},{1,39},{2,0},{3,1},{4,2},{5,3},{6,4},{7,5},{8,46},{9,47},{1... | collective-permute-start | bytes 313352 | tf_op jit(solution)/shard_map/ppermute | solution.py:459
  17.7 0.2 strip.1.strip_ref
  17.9 1.3 %collective-permute-start.5 = (bf16[4,32,128]{2,1,0:T(8,128)(2,1)S(1)}, bf16[4,32,128]{2,1,0:T(8,128)(2,1)S(1)}, u32[]{:S(2)}, u32[]{:S(2)}) collective-permute-start(bf16[4,32,128]{2,1,0:T(8,128)(2,1)S(1)} %strip.1.strip_ref), channel_id=1, source_target_pairs={{32,0},{33,1},{34,2},{35,3},{36,4},{37,5},{38,6},{39,7},{40,8},{41... | collective-permute-start | bytes 98312 | tf_op jit(solution)/shard_map/ppermute | solution.py:466
  19.1 5.8 %collective-permute-done.5.below_ref = bf16[4,32,128]{2,1,0:T(8,128)(2,1)S(1)} collective-permute-done((bf16[4,32,128]{2,1,0:T(8,128)(2,1)S(1)}, bf16[4,32,128]{2,1,0:T(8,128)(2,1)S(1)}, u32[]{:S(2)}, u32[]{:S(2)}) %collective-permute-start.5) | collective-permute-done | bytes 32800 | tf_op jit(solution)/shard_map/ppermute | solution.py:466
  25.0 0.0 collective-permute-done.4.rest_3_
  25.0 0.0 collective-permute-done.3.rest_2_
  25.0 0.0 collective-permute-done.2.rest_1_
  25.0 0.2 make_block.1.rest_0_
  25.2 3.4 %collective-permute-start.8 = (bf16[88,2176]{1,0:T(8,128)(2,1)S(1)}, bf16[88,2176]{1,0:T(8,128)(2,1)S(1)}, u32[]{:S(2)}, u32[]{:S(2)}) collective-permute-start(bf16[88,2176]{1,0:T(8,128)(2,1)S(1)} %make_block.1.rest_0_), channel_id=1, source_target_pairs={{0,16},{1,17},{2,18},{3,19},{4,20},{5,21},{6,22},{7,23},{8,24},{9,... | collective-permute-start | bytes 1148936 | tf_op jit(solution)/shard_map/ppermute | solution.py:459
  28.6 2.4 %collective-permute-start.7 = (bf16[88,2176]{1,0:T(8,128)(2,1)S(1)}, bf16[88,2176]{1,0:T(8,128)(2,1)S(1)}, u32[]{:S(2)}, u32[]{:S(2)}) collective-permute-start(bf16[88,2176]{1,0:T(8,128)(2,1)S(1)} %make_block.1.rest_0_), channel_id=1, source_target_pairs={{0,8},{1,9},{2,10},{3,11},{4,12},{5,13},{6,14},{7,15},{8,16},{9,17... | collective-permute-start | bytes 1148936 | tf_op jit(solution)/shard_map/ppermute | solution.py:459
  31.0 0.3 collective-permute-start.6
  31.3 2.4 %collective-permute-start.9 = (bf16[88,2176]{1,0:T(8,128)(2,1)S(1)}, bf16[88,2176]{1,0:T(8,128)(2,1)S(1)}, u32[]{:S(2)}, u32[]{:S(2)}) collective-permute-start(bf16[88,2176]{1,0:T(8,128)(2,1)S(1)} %make_block.1.rest_0_), channel_id=1, source_target_pairs={{0,1},{1,0},{2,3},{3,2},{4,5},{5,4},{6,7},{7,6},{8,9},{9,8},{10,11... | collective-permute-start | bytes 1148936 | tf_op jit(solution)/shard_map/ppermute | solution.py:459
  33.6 0.2 moved.1
  33.9 5.3 %all_gather.3.window_ref = bf16[4,4,4096]{2,1,0:T(4,128)(2,1)S(1)} all-gather(bf16[1,4,4096]{2,1,0:T(4,128)(2,1)S(1)} %moved.1), channel_id=1, replica_groups={{2,3,4,5},{6,7,8,9},{10,11,12,13},{14,15,16,17},{18,19,20,21},{22,23,24..., dimensions={0}, use_global_device_ids=true | all-gather | bytes 163840 | tf_op jit(solution)/shard_map/all_gather | solution.py:523
  39.2 4.0 %features.1.hidden_ref = bf16[320,4352]{1,0:T(8,128)(2,1)S(1)} custom-call(bf16[4,4,4096]{2,1,0:T(4,128)(2,1)S(1)} %all_gather.3.window_ref, f32[128,384]{1,0:T(8,128)S(1)} %get-tuple-element.34.params_ref), custom_call_target="tpu_custom_call" | custom-call | tf_op jit(solution)/shard_map/features/pallas_call | solution.py:109
  43.2 0.0 collective-permute-done.8.rest_3_
  43.2 2.9 %collective-permute-done.7.rest_2_ = bf16[88,2176]{1,0:T(8,128)(2,1)S(1)} collective-permute-done((bf16[88,2176]{1,0:T(8,128)(2,1)S(1)}, bf16[88,2176]{1,0:T(8,128)(2,1)S(1)}, u32[]{:S(2)}, u32[]{:S(2)}) %collective-permute-start.7) | collective-permute-done | bytes 383008 | tf_op jit(solution)/shard_map/ppermute | solution.py:459
  46.1 1.7 %collective-permute-done.6.rest_1_ = bf16[88,2176]{1,0:T(8,128)(2,1)S(1)} collective-permute-done((bf16[88,2176]{1,0:T(8,128)(2,1)S(1)}, bf16[88,2176]{1,0:T(8,128)(2,1)S(1)}, u32[]{:S(2)}, u32[]{:S(2)}) %collective-permute-start.6) | collective-permute-done | bytes 383008 | tf_op jit(solution)/shard_map/ppermute | solution.py:459
  47.8 1.2 %collective-permute-start.10 = (bf16[88,2176]{1,0:T(8,128)(2,1)S(1)}, bf16[88,2176]{1,0:T(8,128)(2,1)S(1)}, u32[]{:S(2)}, u32[]{:S(2)}) collective-permute-start(bf16[88,2176]{1,0:T(8,128)(2,1)S(1)} %collective-permute-done.6.rest_1_), channel_id=1, source_target_pairs={{0,1},{1,0},{2,3},{3,2},{4,5},{5,4},{6,7},{7,6},{8,9},{9,8},{10,11... | collective-permute-start | bytes 1148936 | tf_op jit(solution)/shard_map/ppermute | solution.py:459
  49.1 0.0 collective-permute-start.11
  49.1 0.5 collective-permute-start.12
  49.6 0.0 collective-permute-done.9.rest_4_
  49.6 0.8 %collective-permute-done.10.rest_5_ = bf16[88,2176]{1,0:T(8,128)(2,1)S(1)} collective-permute-done((bf16[88,2176]{1,0:T(8,128)(2,1)S(1)}, bf16[88,2176]{1,0:T(8,128)(2,1)S(1)}, u32[]{:S(2)}, u32[]{:S(2)}) %collective-permute-start.10) | collective-permute-done | bytes 383008 | tf_op jit(solution)/shard_map/ppermute | solution.py:459
  50.4 0.5 collective-permute-done.11.rest_6_
  51.0 0.5 collective-permute-done.12.rest_7_
  51.5 11.1 %convolve.1 = bf16[320,32,128]{2,1,0:T(8,128)(2,1)} custom-call(bf16[320,4352]{1,0:T(8,128)(2,1)S(1)} %features.1.hidden_ref, bf16[88,2176]{1,0:T(8,128)(2,1)S(1)} %make_block.1.rest_0_, bf16[88,2176]{1,0:T(8,128)(2,1)S(1)} %collective-permute-done.6.rest_1_, bf16[88,2176]{1,0:T(8,128)(2,1)S(1)} %collective-permute-done.7.rest_2_, ...), custom_call_target="tpu_custom_call" | custom-call | tf_op jit(solution)/shard_map/convolve/pallas_call | solution.py:429
  (2 shorter events, 0.0 us)
Async XLA Ops:
  4.2 4.1 %collective-permute-start = (bf16[16,2176]{1,0:T(8,128)(2,1)S(1)}, bf16[16,2176]{1,0:T(8,128)(2,1)S(1)}, u32[]{:S(2)}, u32[]{:S(2)}) collective-permute-start(bf16[16,2176]{1,0:T(8,128)(2,1)S(1)} %get-tuple-element.23), channel_id=1, source_target_pairs={{0,1},{1,0},{2,3},{3,2},{4,5},{5,4},{6,7},{7,6},{8,9},{9,8},{10,11... | collective-permute-start | bytes 208904 | tf_op jit(solution)/shard_map/ppermute | solution.py:459
  5.0 3.3 %collective-permute-start.1 = (bf16[4,32,128]{2,1,0:T(8,128)(2,1)S(1)}, bf16[4,32,128]{2,1,0:T(8,128)(2,1)S(1)}, u32[]{:S(2)}, u32[]{:S(2)}) collective-permute-start(bf16[4,32,128]{2,1,0:T(8,128)(2,1)S(1)} %get-tuple-element.24.own_ref), channel_id=1, source_target_pairs={{1,0},{2,1},{3,2},{4,3},{5,4},{6,5},{7,6},{8,7},{9,8},{10,9},{11,1... | collective-permute-start | bytes 98312 | tf_op jit(solution)/shard_map/ppermute | solution.py:466
  8.4 16.6 %collective-permute-start.4 = (bf16[24,2176]{1,0:T(8,128)(2,1)S(1)}, bf16[24,2176]{1,0:T(8,128)(2,1)S(1)}, u32[]{:S(2)}, u32[]{:S(2)}) collective-permute-start(bf16[24,2176]{1,0:T(8,128)(2,1)S(1)} %pair_up.1.rest_0_), channel_id=1, source_target_pairs={{0,2},{1,3},{2,4},{3,5},{4,6},{5,7},{6,32},{7,33},{8,10},{9,11},{1... | collective-permute-start | bytes 313352 | tf_op jit(solution)/shard_map/ppermute | solution.py:459
  10.1 14.9 %collective-permute-start.3 = (bf16[24,2176]{1,0:T(8,128)(2,1)S(1)}, bf16[24,2176]{1,0:T(8,128)(2,1)S(1)}, u32[]{:S(2)}, u32[]{:S(2)}) collective-permute-start(bf16[24,2176]{1,0:T(8,128)(2,1)S(1)} %pair_up.1.rest_0_), channel_id=1, source_target_pairs={{0,36},{1,37},{2,38},{3,39},{4,0},{5,1},{6,2},{7,3},{8,44},{9,45},... | collective-permute-start | bytes 313352 | tf_op jit(solution)/shard_map/ppermute | solution.py:459
  16.3 8.7 %collective-permute-start.2 = (bf16[24,2176]{1,0:T(8,128)(2,1)S(1)}, bf16[24,2176]{1,0:T(8,128)(2,1)S(1)}, u32[]{:S(2)}, u32[]{:S(2)}) collective-permute-start(bf16[24,2176]{1,0:T(8,128)(2,1)S(1)} %pair_up.1.rest_0_), channel_id=1, source_target_pairs={{0,38},{1,39},{2,0},{3,1},{4,2},{5,3},{6,4},{7,5},{8,46},{9,47},{1... | collective-permute-start | bytes 313352 | tf_op jit(solution)/shard_map/ppermute | solution.py:459
  17.9 7.1 %collective-permute-start.5 = (bf16[4,32,128]{2,1,0:T(8,128)(2,1)S(1)}, bf16[4,32,128]{2,1,0:T(8,128)(2,1)S(1)}, u32[]{:S(2)}, u32[]{:S(2)}) collective-permute-start(bf16[4,32,128]{2,1,0:T(8,128)(2,1)S(1)} %strip.1.strip_ref), channel_id=1, source_target_pairs={{32,0},{33,1},{34,2},{35,3},{36,4},{37,5},{38,6},{39,7},{40,8},{41... | collective-permute-start | bytes 98312 | tf_op jit(solution)/shard_map/ppermute | solution.py:466
  25.2 18.0 %collective-permute-start.8 = (bf16[88,2176]{1,0:T(8,128)(2,1)S(1)}, bf16[88,2176]{1,0:T(8,128)(2,1)S(1)}, u32[]{:S(2)}, u32[]{:S(2)}) collective-permute-start(bf16[88,2176]{1,0:T(8,128)(2,1)S(1)} %make_block.1.rest_0_), channel_id=1, source_target_pairs={{0,16},{1,17},{2,18},{3,19},{4,20},{5,21},{6,22},{7,23},{8,24},{9,... | collective-permute-start | bytes 1148936 | tf_op jit(solution)/shard_map/ppermute | solution.py:459
  28.6 17.6 %collective-permute-start.7 = (bf16[88,2176]{1,0:T(8,128)(2,1)S(1)}, bf16[88,2176]{1,0:T(8,128)(2,1)S(1)}, u32[]{:S(2)}, u32[]{:S(2)}) collective-permute-start(bf16[88,2176]{1,0:T(8,128)(2,1)S(1)} %make_block.1.rest_0_), channel_id=1, source_target_pairs={{0,8},{1,9},{2,10},{3,11},{4,12},{5,13},{6,14},{7,15},{8,16},{9,17... | collective-permute-start | bytes 1148936 | tf_op jit(solution)/shard_map/ppermute | solution.py:459
  31.0 16.9 %collective-permute-start.6 = (bf16[88,2176]{1,0:T(8,128)(2,1)S(1)}, bf16[88,2176]{1,0:T(8,128)(2,1)S(1)}, u32[]{:S(2)}, u32[]{:S(2)}) collective-permute-start(bf16[88,2176]{1,0:T(8,128)(2,1)S(1)} %make_block.1.rest_0_), channel_id=1, source_target_pairs={{0,24},{1,25},{2,26},{3,27},{4,28},{5,29},{6,30},{7,31},{8,0},{9,1... | collective-permute-start | bytes 1148936 | tf_op jit(solution)/shard_map/ppermute | solution.py:459
  31.3 18.3 %collective-permute-start.9 = (bf16[88,2176]{1,0:T(8,128)(2,1)S(1)}, bf16[88,2176]{1,0:T(8,128)(2,1)S(1)}, u32[]{:S(2)}, u32[]{:S(2)}) collective-permute-start(bf16[88,2176]{1,0:T(8,128)(2,1)S(1)} %make_block.1.rest_0_), channel_id=1, source_target_pairs={{0,1},{1,0},{2,3},{3,2},{4,5},{5,4},{6,7},{7,6},{8,9},{9,8},{10,11... | collective-permute-start | bytes 1148936 | tf_op jit(solution)/shard_map/ppermute | solution.py:459
  47.8 2.6 %collective-permute-start.10 = (bf16[88,2176]{1,0:T(8,128)(2,1)S(1)}, bf16[88,2176]{1,0:T(8,128)(2,1)S(1)}, u32[]{:S(2)}, u32[]{:S(2)}) collective-permute-start(bf16[88,2176]{1,0:T(8,128)(2,1)S(1)} %collective-permute-done.6.rest_1_), channel_id=1, source_target_pairs={{0,1},{1,0},{2,3},{3,2},{4,5},{5,4},{6,7},{7,6},{8,9},{9,8},{10,11... | collective-permute-start | bytes 1148936 | tf_op jit(solution)/shard_map/ppermute | solution.py:459
  49.1 1.9 %collective-permute-start.11 = (bf16[88,2176]{1,0:T(8,128)(2,1)S(1)}, bf16[88,2176]{1,0:T(8,128)(2,1)S(1)}, u32[]{:S(2)}, u32[]{:S(2)}) collective-permute-start(bf16[88,2176]{1,0:T(8,128)(2,1)S(1)} %collective-permute-done.7.rest_2_), channel_id=1, source_target_pairs={{0,1},{1,0},{2,3},{3,2},{4,5},{5,4},{6,7},{7,6},{8,9},{9,8},{10,11... | collective-permute-start | bytes 1148936 | tf_op jit(solution)/shard_map/ppermute | solution.py:459
  49.1 2.4 %collective-permute-start.12 = (bf16[88,2176]{1,0:T(8,128)(2,1)S(1)}, bf16[88,2176]{1,0:T(8,128)(2,1)S(1)}, u32[]{:S(2)}, u32[]{:S(2)}) collective-permute-start(bf16[88,2176]{1,0:T(8,128)(2,1)S(1)} %collective-permute-done.8.rest_3_), channel_id=1, source_target_pairs={{0,1},{1,0},{2,3},{3,2},{4,5},{5,4},{6,7},{7,6},{8,9},{9,8},{10,11... | collective-permute-start | bytes 1148936 | tf_op jit(solution)/shard_map/ppermute | solution.py:459

commit v4 on v3

--- a/solution.py
+++ b/solution.py
@@ -118,6 +118,7 @@
 
 
 KPAD = 512
+SPARE = 32
 COLS = 4
 HALF_COLS = 16
 BLOCK = 80
@@ -142,14 +143,14 @@
 LOW = pltpu.CompilerParams(vmem_limit_bytes=8 * 2**20)
 
 
-def prepare_kernel(*rest):
-    w_conv_ref, third_ref, latent_ref, one_ref, two_ref, w_in_ref = rest[15:21]
-    gain_ref, shift_ref, steps_ref = rest[21:24]
-    rows, sems = rest[24:]
-    copies = [pltpu.make_async_copy(rest[i], rest[15 + i], sems.at[i]) for i in range(9)]
+def prepare_kernel(step_ref, *rest):
+    w_conv_ref, third_ref, latent_ref, one_ref, two_ref, w_in_ref = rest[13:19]
+    gain_ref, shift_ref = rest[19:21]
+    rows, sems = rest[21:]
+    copies = [pltpu.make_async_copy(rest[i], rest[13 + i], sems.at[i]) for i in range(8)]
     for copy in copies:
         copy.start()
-    mine_ref, theirs_ref, own_ref, part_ref, params_ref, offsets_ref = rest[9:15]
+    mine_ref, theirs_ref, own_ref, part_ref, params_ref = rest[8:13]
     core, _, _ = position()
     shard, chans = w_conv_ref.shape[1:]
     half, temb_half = chans // 2, third_ref.shape[1] // 2
@@ -160,7 +161,6 @@
     freq = jnp.exp(-jnp.log(jnp.float32(10000.0)) * k / jnp.float32(half))
     for copy in copies:
         copy.wait()
-    offsets_ref[...] = steps_ref[...]
     own_ref[...] = latent_ref[...].astype(jnp.bfloat16)
     for h in range(2):
         for a in range(3):
@@ -180,7 +180,7 @@
         params_ref[at : at + lat, 0:chans] = w_in_ref[tap].astype(jnp.float32)
     params_ref[depth : depth + 1, 0:chans] = gain_ref[...].reshape(1, chans)
     params_ref[depth + 1 : depth + 2, 0:chans] = shift_ref[...].reshape(1, chans)
-    angle = steps_ref[2:3, 0:1].astype(jnp.float32) * freq
+    angle = step_ref[0].astype(jnp.float32) * freq
     emb = jnp.where(lane < half, jnp.cos(angle), jnp.sin(angle))
     first = lax.dot_general(
         emb,
@@ -196,9 +196,9 @@
     part_ref[...] = jnp.where(row == 0, high, jnp.where(row == 1, low, 0.0))
 
 
-def prepare(w_conv, third, latent, w_one, w_two, w_in, gain, shift, steps):
+def prepare(step, w_conv, third, latent, w_one, w_two, w_in, gain, shift):
     wide = 3 * KPAD + third.shape[1] // 2
-    inputs = (w_conv, third, latent, w_one, w_two, w_in, gain, shift, steps)
+    inputs = (w_conv, third, latent, w_one, w_two, w_in, gain, shift)
     inputs = [pltpu.with_memory_space_constraint(v, pltpu.HBM) for v in inputs]
     return pl.pallas_call(
         prepare_kernel,
@@ -208,15 +208,14 @@
             jax.ShapeDtypeStruct(latent.shape, jnp.bfloat16),
             jax.ShapeDtypeStruct((8, w_two.shape[1]), jnp.float32),
             jax.ShapeDtypeStruct((LANES, 3 * LANES), jnp.float32),
-            jax.ShapeDtypeStruct(steps.shape, steps.dtype),
         ),
-        in_specs=[pl.BlockSpec(memory_space=pltpu.HBM)] * len(inputs),
-        out_specs=(VMEM,) * 6,
+        in_specs=[SMEM] + [pl.BlockSpec(memory_space=pltpu.HBM)] * len(inputs),
+        out_specs=(VMEM,) * 5,
         scratch_shapes=[pltpu.VMEM(v.shape, v.dtype) for v in inputs]
         + [pltpu.VMEM((2, 16, wide), jnp.float32), pltpu.SemaphoreType.DMA((len(inputs),))],
         compiler_params=LOW,
         name="prepare",
-    )(*inputs)
+    )(step, *inputs)
 
 
 def pair_kernel(mine_ref, got_ref, time_ref, out_ref, rows):
@@ -255,18 +254,19 @@
         held[(z_lo + k) % 4] = part
     for k in range(4):
         rows[20 * k : 20 * k + 24, :] = held[k]
-    rows[80:88, :] = jnp.zeros((8, rows.shape[1]), jnp.float32)
     high, low = split_float(total)
-    rows[80:81, :temb] = high
-    rows[81:82, :temb] = low
-    out_ref[...] = rows[...].astype(jnp.bfloat16)
+    for q in range(temb // SPARE):
+        piece = slice(q * SPARE, (q + 1) * SPARE)
+        rows[q : q + 1, KPAD - SPARE : KPAD] = high[:, piece]
+        rows[q : q + 1, 2 * KPAD - SPARE : 2 * KPAD] = low[:, piece]
+    out_ref[...] = rows[0:BLOCK, :].astype(jnp.bfloat16)
 
 
 def make_block(parts):
     wide = parts[0].shape[1]
     return pl.pallas_call(
         block_kernel,
-        out_shape=jax.ShapeDtypeStruct((88, wide), jnp.bfloat16),
+        out_shape=jax.ShapeDtypeStruct((BLOCK, wide), jnp.bfloat16),
         in_specs=[VMEM] * 4,
         out_specs=VMEM,
         scratch_shapes=[pltpu.VMEM((4, 24, wide), jnp.float32), pltpu.VMEM((88, wide), jnp.float32)],
@@ -283,7 +283,7 @@
 
 def strip_kernel(offset_ref, own_ref, beside_ref, out_ref):
     width = own_ref.shape[1]
-    chosen = pick(width, 2 * width, offset_ref[1:2, 0:1], True)
+    chosen = pick(width, 2 * width, offset_ref[0], True)
     for c in range(own_ref.shape[0]):
         both = jnp.concatenate([own_ref[c], beside_ref[c]], axis=0)
         out_ref[c] = jnp.dot(chosen, both, preferred_element_type=jnp.float32).astype(jnp.bfloat16)
@@ -291,7 +291,7 @@
 
 def moved_kernel(offset_ref, strip_ref, below_ref, out_ref, stacked, flat):
     lat, width, height = strip_ref.shape
-    chosen = pick(2 * height, height, offset_ref[0:1, 0:1], False)
+    chosen = pick(2 * height, height, offset_ref[0], False)
     for c in range(lat):
         both = jnp.concatenate([strip_ref[c], below_ref[c]], axis=1)
         stacked[c * width : (c + 1) * width, :] = jnp.dot(
@@ -306,11 +306,11 @@
     return pl.pallas_call(
         strip_kernel,
         out_shape=jax.ShapeDtypeStruct(own.shape, own.dtype),
-        in_specs=[VMEM] * 3,
+        in_specs=[SMEM] + [VMEM] * 2,
         out_specs=VMEM,
         compiler_params=LOW,
         name="strip",
-    )(in_vmem(offset), in_vmem(own), in_vmem(beside))
+    )(offset, in_vmem(own), in_vmem(beside))
 
 
 def shift_rows(offset, strip, below):
@@ -318,7 +318,7 @@
     return pl.pallas_call(
         moved_kernel,
         out_shape=jax.ShapeDtypeStruct((1, lat, width * height), strip.dtype),
-        in_specs=[VMEM] * 3,
+        in_specs=[SMEM] + [VMEM] * 2,
         out_specs=VMEM,
         scratch_shapes=[
             pltpu.VMEM((lat * width, height), jnp.float32),
@@ -326,11 +326,11 @@
         ],
         compiler_params=LOW,
         name="moved",
-    )(in_vmem(offset), in_vmem(strip), in_vmem(below))
+    )(offset, in_vmem(strip), in_vmem(below))
 
 
 def conv_kernel(hidden_ref, *rest):
-    refs, (out_ref, prod_a, prod_b, wide, staged, sems) = rest[:8], rest[8:]
+    refs, (out_ref, prod_a, prod_b, wide, staged, line, sems) = rest[:8], rest[8:]
     prods = (prod_a, prod_b)
     core, _, xpos = position()
     chans = hidden_ref.shape[0]
@@ -344,10 +344,14 @@
     def block(side, k, first, last):
         return refs[4 * side + k][0:BLOCK, first:last]
 
-    second = jnp.zeros((1, 2 * temb_half), jnp.float32)
+    spare = jnp.zeros((48, LANES), jnp.float32)
     for ref in refs:
-        two = ref[BLOCK : BLOCK + 8, 0 : 2 * temb_half].astype(jnp.float32)
-        second = second + two[0:1] + two[1:2]
+        for a in range(2):
+            at = (a + 1) * KPAD
+            spare = spare + ref[0:48, at - LANES : at].astype(jnp.float32)
+    for q in range(2 * temb_half // SPARE):
+        line[0:1, q * SPARE : (q + 1) * SPARE] = spare[q : q + 1, LANES - SPARE : LANES]
+    second = line[0:1, :]
     s_two = second / (1.0 + jnp.exp(-second))
     s_two = s_two.astype(jnp.bfloat16).astype(jnp.float32)
     s_low, s_high = s_two[:, :temb_half], s_two[:, temb_half:]
@@ -366,7 +370,7 @@
             for b in range(3):
                 at = (col + b) * LANES
                 right.append(hidden_ref[pl.ds(rows, half), at : at + n])
-            right.append(right[-1][0 : KPAD - 3 * half])
+            right.append(jnp.zeros((SPARE, n), jnp.bfloat16))
         right = jnp.concatenate(right, axis=0)
         left = jnp.concatenate(
             [
@@ -436,6 +440,7 @@
             pltpu.VMEM((3 * chans, COLS * LANES), jnp.float32),
             pltpu.VMEM((chans * HALF_COLS, LANES), jnp.float32),
             pltpu.VMEM((halves, chans, HALF_COLS, LANES), jnp.bfloat16),
+            pltpu.VMEM((8, 1280), jnp.float32),
             pltpu.SemaphoreType.DMA((halves + 3,)),
         ],
         compiler_params=pltpu.CompilerParams(vmem_limit_bytes=20 * 2**20),
@@ -495,9 +500,8 @@
     w_time3,
 ):
     chans = w_in.shape[1]
-    row = lax.broadcasted_iota(jnp.int32, (8, LANES), 0)
-    steps = jnp.where(row == 0, row_offset[:, None], jnp.where(row == 1, col_offset[:, None], timestep[:, None]))
-    mine, theirs, own, part, params, offsets = prepare(
+    mine, theirs, own, part, params = prepare(
+        timestep,
         w_conv,
         w_time3.T,
         latent,
@@ -506,20 +510,19 @@
         w_in.transpose(0, 2, 1),
         norm_gain,
         norm_shift,
-        steps,
     )
     beside = fetch_grid(own, 0, 1)
     got = swap_core(theirs)
     got, beside = lax.optimization_barrier((got, beside))
     zrow = pair_up(mine, got, part)
     near = [zrow, from_z(zrow, 1), from_z(zrow, 2), from_z(zrow, -1)]
-    strip = shift_columns(offsets, own, beside)
+    strip = shift_columns(col_offset, own, beside)
     below = fetch_grid(strip, 1, 0)
     near, below = lax.optimization_barrier((near, below))
     block = make_block(near)
     after, before, across = from_x(block, 1), from_x(block, -1), from_x(block, 2)
 
-    moved = shift_rows(offsets, strip, below)
+    moved = shift_rows(row_offset, strip, below)
     window = lax.all_gather(
         moved, ("row", "col"), axis_index_groups=WINDOW_GROUPS, axis=0, tiled=True
     )

time: 62.9 us -> 59.3 us (0.943)
  the two profiles are of different devices: /device:TPU:49 before, /device:TPU:1 now
where the time goes in v4:
time: 59.3 us; the launch traced here: 58.8 us
  starting transfers between devices  21.8 us (37%)
  Pallas kernels  17.3 us (29%)
  blocking collectives  9.48 us (16%)
  waiting for transfers between devices  8.09 us (14%)
  between operations  2.19 us (4%)
    ppermute x11, starting transfers between devices, send(): return lax.ppermute(value, ('row', 'col'), pairs_of(move))  17.9 us
    pallas_call x1, Pallas kernels, conv(): pl.pallas_call(conv_kernel, out_shape=jax.ShapeDtypeStruct((chans, width,...  11.1 us
    all_gather x1, blocking collectives, body(): lax.all_gather(moved, ('row', 'col'), axis_index_groups=WINDOW_GROUPS, ax...  9.48 us
    ppermute x2, waiting for transfers between devices, fetch_grid(): return lax.ppermute(value, ('row', 'col'), pairs)  6.1 us
    pallas_call x1, Pallas kernels, features(): pl.pallas_call(features_kernel, out_shape=jax.ShapeDtypeStruct((chans, (w...  4.03 us
    ppermute x2, starting transfers between devices, fetch_grid(): return lax.ppermute(value, ('row', 'col'), pairs)  3.92 us
    ppermute x11, waiting for transfers between devices, send(): return lax.ppermute(value, ('row', 'col'), pairs_of(move))  1.99 us
    pallas_call x1, Pallas kernels, prepare(): pl.pallas_call(prepare_kernel, out_shape=(jax.ShapeDtypeStruct((16, wide)...  1.51 us
  transfers between devices with their start and end apart: 13, of which 5 were waited for; matrix products, arithmetic and copies ran while one was open for 0% of the time, Pallas kernels for 7%

profile of v4, /device:TPU:1, one launch (start us, length us, event | category | flops | bytes accessed | tf_op | source)
XLA Modules:
  0.0 58.8 jit_solution(18398572580511629722)
XLA Ops:
  0.7 1.5 %prepare.1 = (bf16[16,2176]{1,0:T(8,128)(2,1)S(1)}, bf16[16,2176]{1,0:T(8,128)(2,1)S(1)}, bf16[4,32,128]{2,1,0:T(8,128)(2,1)S(1)}, f32[8,1280]{1,0:T(8,128)S(1)}, f32[128,384]{1,0:T(8,128)S(1)}) custom-call(s32[1]{0:T(128)S(6)} %copy.14.step_ref, bf16[9,10,320]{2,1,0:T(8,128)(2,1)} %rest_0_.1, bf16[10,1280]{1,0:T(8,128)(2,1)} %bitcast.3, ...), custom_call_target="tpu_custom_call" | custom-call | tf_op jit(solution)/shard_map/prepare/pallas_call | solution.py:203
  2.2 3.3 %collective-permute-start = (bf16[16,2176]{1,0:T(8,128)(2,1)S(1)}, bf16[16,2176]{1,0:T(8,128)(2,1)S(1)}, u32[]{:S(2)}, u32[]{:S(2)}) collective-permute-start(bf16[16,2176]{1,0:T(8,128)(2,1)S(1)} %get-tuple-element.22), channel_id=1, source_target_pairs={{0,1},{1,0},{2,3},{3,2},{4,5},{5,4},{6,7},{7,6},{8,9},{9,8},{10,11... | collective-permute-start | bytes 208904 | tf_op jit(solution)/shard_map/ppermute | solution.py:464
  5.5 0.1 collective-permute-start.1
  5.6 3.2 %collective-permute-done.1.beside_ref = bf16[4,32,128]{2,1,0:T(8,128)(2,1)S(1)} collective-permute-done((bf16[4,32,128]{2,1,0:T(8,128)(2,1)S(1)}, bf16[4,32,128]{2,1,0:T(8,128)(2,1)S(1)}, u32[]{:S(2)}, u32[]{:S(2)}) %collective-permute-start.1) | collective-permute-done | bytes 32800 | tf_op jit(solution)/shard_map/ppermute | solution.py:471
  8.8 0.0 collective-permute-done.got_ref
  8.8 0.1 pair_up.1.rest_0_
  8.9 0.1 collective-permute-start.4
  9.0 7.7 %collective-permute-start.3 = (bf16[24,2176]{1,0:T(8,128)(2,1)S(1)}, bf16[24,2176]{1,0:T(8,128)(2,1)S(1)}, u32[]{:S(2)}, u32[]{:S(2)}) collective-permute-start(bf16[24,2176]{1,0:T(8,128)(2,1)S(1)} %pair_up.1.rest_0_), channel_id=1, source_target_pairs={{0,36},{1,37},{2,38},{3,39},{4,0},{5,1},{6,2},{7,3},{8,44},{9,45},... | collective-permute-start | bytes 313352 | tf_op jit(solution)/shard_map/ppermute | solution.py:464
  16.7 0.0 collective-permute-start.2
  17.4 0.1 strip.1.strip_ref
  17.5 3.8 %collective-permute-start.5 = (bf16[4,32,128]{2,1,0:T(8,128)(2,1)S(1)}, bf16[4,32,128]{2,1,0:T(8,128)(2,1)S(1)}, u32[]{:S(2)}, u32[]{:S(2)}) collective-permute-start(bf16[4,32,128]{2,1,0:T(8,128)(2,1)S(1)} %strip.1.strip_ref), channel_id=1, source_target_pairs={{32,0},{33,1},{34,2},{35,3},{36,4},{37,5},{38,6},{39,7},{40,8},{41... | collective-permute-start | bytes 98312 | tf_op jit(solution)/shard_map/ppermute | solution.py:471
  21.3 2.9 %collective-permute-done.5.below_ref = bf16[4,32,128]{2,1,0:T(8,128)(2,1)S(1)} collective-permute-done((bf16[4,32,128]{2,1,0:T(8,128)(2,1)S(1)}, bf16[4,32,128]{2,1,0:T(8,128)(2,1)S(1)}, u32[]{:S(2)}, u32[]{:S(2)}) %collective-permute-start.5) | collective-permute-done | bytes 32800 | tf_op jit(solution)/shard_map/ppermute | solution.py:471
  24.2 0.0 collective-permute-done.4.rest_3_
  24.2 0.0 collective-permute-done.3.rest_2_
  24.2 0.0 collective-permute-done.2.rest_1_
  24.2 0.2 make_block.1.rest_0_
  24.4 2.8 %collective-permute-start.8 = (bf16[80,2176]{1,0:T(8,128)(2,1)S(1)}, bf16[80,2176]{1,0:T(8,128)(2,1)S(1)}, u32[]{:S(2)}, u32[]{:S(2)}) collective-permute-start(bf16[80,2176]{1,0:T(8,128)(2,1)S(1)} %make_block.1.rest_0_), channel_id=1, source_target_pairs={{0,16},{1,17},{2,18},{3,19},{4,20},{5,21},{6,22},{7,23},{8,24},{9,... | collective-permute-start | bytes 1044488 | tf_op jit(solution)/shard_map/ppermute | solution.py:464
  27.2 1.9 %collective-permute-start.7 = (bf16[80,2176]{1,0:T(8,128)(2,1)S(1)}, bf16[80,2176]{1,0:T(8,128)(2,1)S(1)}, u32[]{:S(2)}, u32[]{:S(2)}) collective-permute-start(bf16[80,2176]{1,0:T(8,128)(2,1)S(1)} %make_block.1.rest_0_), channel_id=1, source_target_pairs={{0,8},{1,9},{2,10},{3,11},{4,12},{5,13},{6,14},{7,15},{8,16},{9,17... | collective-permute-start | bytes 1044488 | tf_op jit(solution)/shard_map/ppermute | solution.py:464
  29.1 0.8 %collective-permute-start.6 = (bf16[80,2176]{1,0:T(8,128)(2,1)S(1)}, bf16[80,2176]{1,0:T(8,128)(2,1)S(1)}, u32[]{:S(2)}, u32[]{:S(2)}) collective-permute-start(bf16[80,2176]{1,0:T(8,128)(2,1)S(1)} %make_block.1.rest_0_), channel_id=1, source_target_pairs={{0,24},{1,25},{2,26},{3,27},{4,28},{5,29},{6,30},{7,31},{8,0},{9,1... | collective-permute-start | bytes 1044488 | tf_op jit(solution)/shard_map/ppermute | solution.py:464
  30.6 0.3 collective-permute-start.9
  30.9 0.2 moved.1
  31.1 9.5 %all_gather.3.window_ref = bf16[4,4,4096]{2,1,0:T(4,128)(2,1)S(1)} all-gather(bf16[1,4,4096]{2,1,0:T(4,128)(2,1)S(1)} %moved.1), channel_id=1, replica_groups={{2,3,4,5},{6,7,8,9},{10,11,12,13},{14,15,16,17},{18,19,20,21},{22,23,24..., dimensions={0}, use_global_device_ids=true | all-gather | bytes 163840 | tf_op jit(solution)/shard_map/all_gather | solution.py:526
  40.6 4.0 %features.1.hidden_ref = bf16[320,4352]{1,0:T(8,128)(2,1)S(1)} custom-call(bf16[4,4,4096]{2,1,0:T(4,128)(2,1)S(1)} %all_gather.3.window_ref, f32[128,384]{1,0:T(8,128)S(1)} %get-tuple-element.32.params_ref), custom_call_target="tpu_custom_call" | custom-call | tf_op jit(solution)/shard_map/features/pallas_call | solution.py:109
  44.6 0.0 collective-permute-done.8.rest_3_
  44.6 0.0 collective-permute-done.7.rest_2_
  44.7 0.0 collective-permute-done.6.rest_1_
  44.7 0.4 collective-permute-start.10
  45.1 0.3 collective-permute-start.11
  45.4 0.2 collective-permute-start.12
  45.6 0.0 collective-permute-done.9.rest_4_
  45.6 1.0 %collective-permute-done.10.rest_5_ = bf16[80,2176]{1,0:T(8,128)(2,1)S(1)} collective-permute-done((bf16[80,2176]{1,0:T(8,128)(2,1)S(1)}, bf16[80,2176]{1,0:T(8,128)(2,1)S(1)}, u32[]{:S(2)}, u32[]{:S(2)}) %collective-permute-start.10) | collective-permute-done | bytes 348192 | tf_op jit(solution)/shard_map/ppermute | solution.py:464
  46.6 0.5 collective-permute-done.11.rest_6_
  47.1 0.5 collective-permute-done.12.rest_7_
  47.6 11.1 %convolve.1 = bf16[320,32,128]{2,1,0:T(8,128)(2,1)} custom-call(bf16[320,4352]{1,0:T(8,128)(2,1)S(1)} %features.1.hidden_ref, bf16[80,2176]{1,0:T(8,128)(2,1)S(1)} %make_block.1.rest_0_, bf16[80,2176]{1,0:T(8,128)(2,1)S(1)} %collective-permute-done.6.rest_1_, bf16[80,2176]{1,0:T(8,128)(2,1)S(1)} %collective-permute-done.7.rest_2_, ...), custom_call_target="tpu_custom_call" | custom-call | tf_op jit(solution)/shard_map/convolve/pallas_call | solution.py:433
Async XLA Ops:
  2.2 6.7 %collective-permute-start = (bf16[16,2176]{1,0:T(8,128)(2,1)S(1)}, bf16[16,2176]{1,0:T(8,128)(2,1)S(1)}, u32[]{:S(2)}, u32[]{:S(2)}) collective-permute-start(bf16[16,2176]{1,0:T(8,128)(2,1)S(1)} %get-tuple-element.22), channel_id=1, source_target_pairs={{0,1},{1,0},{2,3},{3,2},{4,5},{5,4},{6,7},{7,6},{8,9},{9,8},{10,11... | collective-permute-start | bytes 208904 | tf_op jit(solution)/shard_map/ppermute | solution.py:464
  5.5 3.3 %collective-permute-start.1 = (bf16[4,32,128]{2,1,0:T(8,128)(2,1)S(1)}, bf16[4,32,128]{2,1,0:T(8,128)(2,1)S(1)}, u32[]{:S(2)}, u32[]{:S(2)}) collective-permute-start(bf16[4,32,128]{2,1,0:T(8,128)(2,1)S(1)} %get-tuple-element.23.own_ref), channel_id=1, source_target_pairs={{1,0},{2,1},{3,2},{4,3},{5,4},{6,5},{7,6},{8,7},{9,8},{10,9},{11,1... | collective-permute-start | bytes 98312 | tf_op jit(solution)/shard_map/ppermute | solution.py:471
  8.9 15.3 %collective-permute-start.4 = (bf16[24,2176]{1,0:T(8,128)(2,1)S(1)}, bf16[24,2176]{1,0:T(8,128)(2,1)S(1)}, u32[]{:S(2)}, u32[]{:S(2)}) collective-permute-start(bf16[24,2176]{1,0:T(8,128)(2,1)S(1)} %pair_up.1.rest_0_), channel_id=1, source_target_pairs={{0,2},{1,3},{2,4},{3,5},{4,6},{5,7},{6,32},{7,33},{8,10},{9,11},{1... | collective-permute-start | bytes 313352 | tf_op jit(solution)/shard_map/ppermute | solution.py:464
  9.0 15.2 %collective-permute-start.3 = (bf16[24,2176]{1,0:T(8,128)(2,1)S(1)}, bf16[24,2176]{1,0:T(8,128)(2,1)S(1)}, u32[]{:S(2)}, u32[]{:S(2)}) collective-permute-start(bf16[24,2176]{1,0:T(8,128)(2,1)S(1)} %pair_up.1.rest_0_), channel_id=1, source_target_pairs={{0,36},{1,37},{2,38},{3,39},{4,0},{5,1},{6,2},{7,3},{8,44},{9,45},... | collective-permute-start | bytes 313352 | tf_op jit(solution)/shard_map/ppermute | solution.py:464
  16.7 7.5 %collective-permute-start.2 = (bf16[24,2176]{1,0:T(8,128)(2,1)S(1)}, bf16[24,2176]{1,0:T(8,128)(2,1)S(1)}, u32[]{:S(2)}, u32[]{:S(2)}) collective-permute-start(bf16[24,2176]{1,0:T(8,128)(2,1)S(1)} %pair_up.1.rest_0_), channel_id=1, source_target_pairs={{0,38},{1,39},{2,0},{3,1},{4,2},{5,3},{6,4},{7,5},{8,46},{9,47},{1... | collective-permute-start | bytes 313352 | tf_op jit(solution)/shard_map/ppermute | solution.py:464
  17.5 6.7 %collective-permute-start.5 = (bf16[4,32,128]{2,1,0:T(8,128)(2,1)S(1)}, bf16[4,32,128]{2,1,0:T(8,128)(2,1)S(1)}, u32[]{:S(2)}, u32[]{:S(2)}) collective-permute-start(bf16[4,32,128]{2,1,0:T(8,128)(2,1)S(1)} %strip.1.strip_ref), channel_id=1, source_target_pairs={{32,0},{33,1},{34,2},{35,3},{36,4},{37,5},{38,6},{39,7},{40,8},{41... | collective-permute-start | bytes 98312 | tf_op jit(solution)/shard_map/ppermute | solution.py:471
  24.4 20.2 %collective-permute-start.8 = (bf16[80,2176]{1,0:T(8,128)(2,1)S(1)}, bf16[80,2176]{1,0:T(8,128)(2,1)S(1)}, u32[]{:S(2)}, u32[]{:S(2)}) collective-permute-start(bf16[80,2176]{1,0:T(8,128)(2,1)S(1)} %make_block.1.rest_0_), channel_id=1, source_target_pairs={{0,16},{1,17},{2,18},{3,19},{4,20},{5,21},{6,22},{7,23},{8,24},{9,... | collective-permute-start | bytes 1044488 | tf_op jit(solution)/shard_map/ppermute | solution.py:464
  27.2 17.4 %collective-permute-start.7 = (bf16[80,2176]{1,0:T(8,128)(2,1)S(1)}, bf16[80,2176]{1,0:T(8,128)(2,1)S(1)}, u32[]{:S(2)}, u32[]{:S(2)}) collective-permute-start(bf16[80,2176]{1,0:T(8,128)(2,1)S(1)} %make_block.1.rest_0_), channel_id=1, source_target_pairs={{0,8},{1,9},{2,10},{3,11},{4,12},{5,13},{6,14},{7,15},{8,16},{9,17... | collective-permute-start | bytes 1044488 | tf_op jit(solution)/shard_map/ppermute | solution.py:464
  29.1 15.5 %collective-permute-start.6 = (bf16[80,2176]{1,0:T(8,128)(2,1)S(1)}, bf16[80,2176]{1,0:T(8,128)(2,1)S(1)}, u32[]{:S(2)}, u32[]{:S(2)}) collective-permute-start(bf16[80,2176]{1,0:T(8,128)(2,1)S(1)} %make_block.1.rest_0_), channel_id=1, source_target_pairs={{0,24},{1,25},{2,26},{3,27},{4,28},{5,29},{6,30},{7,31},{8,0},{9,1... | collective-permute-start | bytes 1044488 | tf_op jit(solution)/shard_map/ppermute | solution.py:464
  30.6 15.0 %collective-permute-start.9 = (bf16[80,2176]{1,0:T(8,128)(2,1)S(1)}, bf16[80,2176]{1,0:T(8,128)(2,1)S(1)}, u32[]{:S(2)}, u32[]{:S(2)}) collective-permute-start(bf16[80,2176]{1,0:T(8,128)(2,1)S(1)} %make_block.1.rest_0_), channel_id=1, source_target_pairs={{0,1},{1,0},{2,3},{3,2},{4,5},{5,4},{6,7},{7,6},{8,9},{9,8},{10,11... | collective-permute-start | bytes 1044488 | tf_op jit(solution)/shard_map/ppermute | solution.py:464
  44.7 1.9 %collective-permute-start.10 = (bf16[80,2176]{1,0:T(8,128)(2,1)S(1)}, bf16[80,2176]{1,0:T(8,128)(2,1)S(1)}, u32[]{:S(2)}, u32[]{:S(2)}) collective-permute-start(bf16[80,2176]{1,0:T(8,128)(2,1)S(1)} %collective-permute-done.6.rest_1_), channel_id=1, source_target_pairs={{0,1},{1,0},{2,3},{3,2},{4,5},{5,4},{6,7},{7,6},{8,9},{9,8},{10,11... | collective-permute-start | bytes 1044488 | tf_op jit(solution)/shard_map/ppermute | solution.py:464
  45.1 2.0 %collective-permute-start.11 = (bf16[80,2176]{1,0:T(8,128)(2,1)S(1)}, bf16[80,2176]{1,0:T(8,128)(2,1)S(1)}, u32[]{:S(2)}, u32[]{:S(2)}) collective-permute-start(bf16[80,2176]{1,0:T(8,128)(2,1)S(1)} %collective-permute-done.7.rest_2_), channel_id=1, source_target_pairs={{0,1},{1,0},{2,3},{3,2},{4,5},{5,4},{6,7},{7,6},{8,9},{9,8},{10,11... | collective-permute-start | bytes 1044488 | tf_op jit(solution)/shard_map/ppermute | solution.py:464
  45.4 2.1 %collective-permute-start.12 = (bf16[80,2176]{1,0:T(8,128)(2,1)S(1)}, bf16[80,2176]{1,0:T(8,128)(2,1)S(1)}, u32[]{:S(2)}, u32[]{:S(2)}) collective-permute-start(bf16[80,2176]{1,0:T(8,128)(2,1)S(1)} %collective-permute-done.8.rest_3_), channel_id=1, source_target_pairs={{0,1},{1,0},{2,3},{3,2},{4,5},{5,4},{6,7},{7,6},{8,9},{9,8},{10,11... | collective-permute-start | bytes 1044488 | tf_op jit(solution)/shard_map/ppermute | solution.py:464
